TPU v7x, 32 devices: a whole 2x2x4 slice. The times are simulated.
32 devices in a mesh: fsdp: 4 (over y, x), context: 2 (over core), expert: 4 (over z).
Axes of the slice: x: 2, y: 2, z: 4, core: 2. Of those that a mesh axis runs over, the one named last changes fastest.
Arguments:
- tokens: bfloat16 [16, 1024, 768], P(('fsdp', 'expert'), 'context'), may hold values from -6 to 6
- cotangent: bfloat16 [16, 1024, 768], P(('fsdp', 'expert'), 'context'), may hold values from -6 to 6
- expert_ids: int32 [16, 1024], P(('fsdp', 'expert'), 'context'), may hold values from 0 to 3, as said below
- capacity_slot: int32 [16, 1024], P(('fsdp', 'expert'), 'context'), may hold values from -1 to 159, as said below
- buckets: int32 [2047], replicated, may hold values from 0 to 31, as said below
- attn_gain: bfloat16 [768], P('fsdp'), may hold values from 0.25 to 1.75
- query_weight: bfloat16 [768, 768], P('fsdp'), may hold values from -0.0390625 to 0.0390625
- key_weight: bfloat16 [768, 768], P('fsdp'), may hold values from -0.21875 to 0.21875
- value_weight: bfloat16 [768, 768], P('fsdp'), may hold values from -0.21875 to 0.21875
- attention_output_matrix: bfloat16 [768, 768], P('fsdp'), may hold values from -2 to 2
- bias_table: bfloat16 [32, 12], P('fsdp'), may hold values from -4 to 4
- mixture_gain: bfloat16 [768], P('fsdp'), may hold values from 0.25 to 1.75
- router_matrix: bfloat16 [768, 4], P('fsdp'), may hold values from -0.15625 to 0.15625
- expert_in: bfloat16 [4, 768, 3072], P('expert', 'fsdp'), may hold values from -0.21875 to 0.21875
- expert_out: bfloat16 [4, 3072, 768], P('expert', 'fsdp'), may hold values from -0.625 to 0.625
Outputs:
- layer_out: bfloat16 [16, 1024, 768], P(('fsdp', 'expert'), 'context')
- tokens_grad: bfloat16 [16, 1024, 768], P(('fsdp', 'expert'), 'context')
- attn_gain_grad: float32 [768], P('fsdp')
- query_grad: float32 [768, 768], P('fsdp')
- key_grad: float32 [768, 768], P('fsdp')
- value_grad: float32 [768, 768], P('fsdp')
- output_grad: float32 [768, 768], P('fsdp')
- bias_grad: float32 [32, 12], P('fsdp')
- mixture_gain_grad: float32 [768], P('fsdp')
- router_grad: float32 [768, 4], P('fsdp')
- expert_in_grad: float32 [4, 768, 3072], P('expert', 'fsdp')
- expert_out_grad: float32 [4, 3072, 768], P('expert', 'fsdp')
Inputs may be any that keep to these rules, and one draw needn't show every extreme that they name: `expert_ids`: on every device some expert is named by more than 160 of its 512 tokens. `capacity_slot`: among one device's tokens of one expert, the kept ones hold distinct slots 0 to their count - 1, at most 160 of them; a token is dropped (-1) only where its expert holds 160 kept tokens of that device; on every device some expert fills all 160 slots. Entry j - i + 1023 is the bucket of key j for query i: offsets up to 0 get buckets below 16, positive offsets 32 / 2 and above, never falling as the distance grows on either side.
All inputs are finite; a program needn't handle non-finite values.
Results may differ from a plain program's by a relative error of at most 0.018.
Values may be sent and summed in bfloat16 or wider, within the bound.
A program may use at most 256 MiB of HBM per device.

v0:
```python
import jax
import jax.numpy as jnp
from jax import lax
from jax.sharding import PartitionSpec as P

highest_score = lax.Precision.HIGHEST
epsilon = 1e-06


def rms_norm(values, norm_gain):
    return (
        values * lax.rsqrt(jnp.mean(values * values, axis=-1, keepdims=True) + epsilon) * norm_gain
    )


def smooth(values):
    return jax.nn.gelu(values, approximate=True)


def per_device(
    tokens,
    cotangent,
    expert_ids,
    capacity_slot,
    buckets,
    attn_gain,
    query_weight,
    key_weight,
    value_weight,
    attention_output_matrix,
    bias_table,
    mixture_gain,
    router_matrix,
    expert_in,
    expert_out,
):
    row_count = tokens.shape[1]
    model_width = tokens.shape[2]
    inputs = tokens.reshape(row_count, model_width).astype(jnp.float32)
    upstream = cotangent.reshape(row_count, model_width).astype(jnp.float32)
    chosen = expert_ids.reshape(row_count)
    slot_ids = capacity_slot.reshape(row_count)
    seq_length = (buckets.shape[0] + 1) // 2
    (
        gain_one,
        w_query,
        w_key,
        w_value,
        w_output,
        table_rows,
        gain_two,
        w_router,
        w_first,
        w_second,
    ) = (
        lax.all_gather(attn_gain, "fsdp", axis=0, tiled=True),
        lax.all_gather(query_weight, "fsdp", axis=0, tiled=True),
        lax.all_gather(key_weight, "fsdp", axis=0, tiled=True),
        lax.all_gather(value_weight, "fsdp", axis=0, tiled=True),
        lax.all_gather(attention_output_matrix, "fsdp", axis=0, tiled=True),
        lax.all_gather(bias_table, "fsdp", axis=0, tiled=True),
        lax.all_gather(mixture_gain, "fsdp", axis=0, tiled=True),
        lax.all_gather(router_matrix, "fsdp", axis=0, tiled=True),
        lax.all_gather(expert_in, "fsdp", axis=1, tiled=True),
        lax.all_gather(expert_out, "fsdp", axis=1, tiled=True),
    )
    head_count = table_rows.shape[1]
    head_dim = model_width // head_count
    bucket_count = table_rows.shape[0]
    normalized_input, norm_one_back = jax.vjp(rms_norm, inputs, gain_one.astype(jnp.float32))
    hidden = normalized_input.astype(jnp.bfloat16)
    query_rows = jnp.dot(hidden, w_query, preferred_element_type=jnp.float32).astype(jnp.bfloat16)
    key_rows = jnp.dot(hidden, w_key, preferred_element_type=jnp.float32).astype(jnp.bfloat16)
    value_rows = jnp.dot(hidden, w_value, preferred_element_type=jnp.float32).astype(jnp.bfloat16)
    keys_all, values_all = (
        lax.all_gather(key_rows, "context", axis=0, tiled=True),
        lax.all_gather(value_rows, "context", axis=0, tiled=True),
    )
    first_row = lax.axis_index("context") * row_count
    bucket_ids = jnp.arange(bucket_count, dtype=jnp.int32)
    block_size = min(512, seq_length)
    block_count = seq_length // block_size
    query_heads = query_rows.reshape(row_count, head_count, head_dim)
    offset_onehot = (buckets[:, None] == bucket_ids).astype(jnp.float32)
    table_by_offset = jnp.einsum(
        "ob,bh->ho", offset_onehot, table_rows.astype(jnp.float32), precision=highest_score
    ).astype(jnp.bfloat16)

    def bias_block(query_first, query_count, key_first, key_count):
        width = query_count + key_count - 1
        window = lax.dynamic_slice_in_dim(
            table_by_offset, key_first - query_first + seq_length - query_count, width, 1
        )
        repeated = jnp.tile(window, (1, query_count + 1))
        skewed = lax.slice_in_dim(
            repeated, query_count - 1, query_count - 1 + query_count * (width - 1), axis=1
        )
        return skewed.reshape(head_count, query_count, width - 1)[:, :, :key_count]

    def table_terms(grad_scores, query_first, key_first):
        query_count = grad_scores.shape[1]
        key_count = grad_scores.shape[2]
        width = query_count + key_count - 1
        flipped = grad_scores.astype(jnp.float32)[:, ::-1, :]
        padded = jnp.pad(flipped, ((0, 0), (0, 0), (0, query_count)))
        flat = padded.reshape(head_count, query_count * (key_count + query_count))[
            :, : query_count * width
        ]
        diagonal_sums = jnp.sum(flat.reshape(head_count, query_count, width), axis=1)
        bucket_rows = lax.dynamic_slice_in_dim(
            buckets, key_first - query_first + seq_length - query_count, width, 0
        )
        window_onehot = (bucket_rows[:, None] == bucket_ids).astype(jnp.float32)
        return jnp.einsum("hw,wb->bh", diagonal_sums, window_onehot, precision=highest_score)

    def key_block(block_index):
        return lax.dynamic_slice_in_dim(keys_all, block_index * block_size, block_size, 0).reshape(
            block_size, head_count, head_dim
        )

    def value_block(block_index):
        return lax.dynamic_slice_in_dim(
            values_all, block_index * block_size, block_size, 0
        ).reshape(block_size, head_count, head_dim)

    def scores_at(block_index):
        raw = jnp.einsum(
            "qhd,khd->hqk", query_heads, key_block(block_index), preferred_element_type=jnp.float32
        )
        bias_part = bias_block(first_row, row_count, block_index * block_size, block_size)
        return raw + bias_part.astype(jnp.float32)

    def max_sum(state_pair, block_index):
        running_max, running_sum = state_pair
        scores = scores_at(block_index)
        new_max = jnp.maximum(running_max, jnp.max(scores, axis=-1))
        running_sum = running_sum * jnp.exp(running_max - new_max) + jnp.sum(
            jnp.exp(scores - new_max[..., None]), axis=-1
        )
        return ((new_max, running_sum), None)

    start_pair = (
        jnp.full((head_count, row_count), -1e30, jnp.float32),
        jnp.zeros((head_count, row_count), jnp.float32),
    )
    (running_max, running_sum), _ = lax.scan(max_sum, start_pair, jnp.arange(block_count))
    log_total = running_max + jnp.log(running_sum)

    def weighted(accumulated, block_index):
        probabilities = jnp.exp(scores_at(block_index) - log_total[..., None]).astype(jnp.bfloat16)
        update = jnp.einsum(
            "hqk,khd->qhd",
            probabilities,
            value_block(block_index),
            preferred_element_type=jnp.float32,
        )
        return (accumulated + update, None)

    attention_result, _ = lax.scan(
        weighted, jnp.zeros((row_count, head_count, head_dim), jnp.float32), jnp.arange(block_count)
    )
    attention_result = attention_result.reshape(row_count, model_width)
    attended_low = attention_result.astype(jnp.bfloat16)
    middle = inputs + jnp.dot(attended_low, w_output, preferred_element_type=jnp.float32)
    experts = w_router.shape[1]
    expert_groups = lax.axis_size("expert")
    local_experts = w_first.shape[0]
    capacity = row_count * 5 // (4 * experts)
    normed_two, norm_two_back = jax.vjp(rms_norm, middle, gain_two.astype(jnp.float32))
    second_hidden = normed_two.astype(jnp.bfloat16)
    router_logits = jnp.dot(second_hidden, w_router, preferred_element_type=jnp.float32)
    shifted = router_logits - jnp.max(router_logits, axis=-1, keepdims=True)
    raised = jnp.exp(shifted)
    router_probs = raised / jnp.sum(raised, axis=-1, keepdims=True)
    selector = (chosen[:, None] == jnp.arange(experts, dtype=jnp.int32)).astype(jnp.float32)
    gate_value = jnp.sum(router_probs * selector, axis=-1)
    position = chosen * capacity + slot_ids
    dispatch = (
        (position[:, None] == jnp.arange(experts * capacity, dtype=jnp.int32))
        & (slot_ids[:, None] >= 0)
    ).astype(jnp.bfloat16)
    outgoing = jnp.einsum("tc,td->cd", dispatch, second_hidden, preferred_element_type=jnp.float32)
    outgoing = outgoing.astype(jnp.bfloat16).reshape(
        expert_groups, local_experts, capacity, model_width
    )
    received = lax.all_to_all(outgoing, "expert", split_axis=0, concat_axis=0, tiled=True)
    pre_act = jnp.einsum("sxcd,xdf->sxcf", received, w_first, preferred_element_type=jnp.float32)
    activated = smooth(pre_act).astype(jnp.bfloat16)
    produced = jnp.einsum(
        "sxcf,xfd->sxcd", activated, w_second, preferred_element_type=jnp.float32
    ).astype(jnp.bfloat16)
    returned = lax.all_to_all(produced, "expert", split_axis=0, concat_axis=0, tiled=True)
    returned, received, pre_act = (returned, received, pre_act)
    combined = jnp.einsum(
        "tc,cd->td",
        dispatch,
        returned.reshape(experts * capacity, model_width),
        preferred_element_type=jnp.float32,
    )
    layer_sum = middle + gate_value[:, None] * combined
    grad_gate = jnp.sum(upstream * combined, axis=-1)
    weighted_grad = (gate_value[:, None] * upstream).astype(jnp.bfloat16)
    grad_slots = jnp.einsum(
        "tc,td->cd", dispatch, weighted_grad, preferred_element_type=jnp.float32
    )
    grad_slots = grad_slots.astype(jnp.bfloat16).reshape(
        expert_groups, local_experts, capacity, model_width
    )
    grad_produced = lax.all_to_all(grad_slots, "expert", split_axis=0, concat_axis=0, tiled=True)
    grad_act = jnp.einsum(
        "sxcd,xfd->sxcf", grad_produced, w_second, preferred_element_type=jnp.float32
    )
    activated_again, smooth_back = jax.vjp(smooth, pre_act)
    grad_pre = smooth_back(grad_act)[0].astype(jnp.bfloat16)
    second_grad = jnp.einsum(
        "sxcf,sxcd->xfd",
        activated_again.astype(jnp.bfloat16),
        grad_produced,
        preferred_element_type=jnp.float32,
    )
    first_grad = jnp.einsum(
        "sxcd,sxcf->xdf", received, grad_pre, preferred_element_type=jnp.float32
    )
    grad_received = jnp.einsum(
        "sxcf,xdf->sxcd", grad_pre, w_first, preferred_element_type=jnp.float32
    ).astype(jnp.bfloat16)
    grad_sent = lax.all_to_all(grad_received, "expert", split_axis=0, concat_axis=0, tiled=True)
    grad_hidden_two = jnp.einsum(
        "tc,cd->td",
        dispatch,
        grad_sent.reshape(experts * capacity, model_width),
        preferred_element_type=jnp.float32,
    )
    grad_logits = router_probs * (selector - gate_value[:, None]) * grad_gate[:, None]
    router_grad = jnp.einsum(
        "td,te->de", second_hidden.astype(jnp.float32), grad_logits, precision=highest_score
    )
    grad_hidden_two = grad_hidden_two + jnp.einsum(
        "te,de->td", grad_logits, w_router.astype(jnp.float32), precision=highest_score
    )
    grad_middle_norm, gain_two_grad = norm_two_back(grad_hidden_two)
    grad_middle = upstream + grad_middle_norm
    grad_branch = grad_middle.astype(jnp.bfloat16)
    output_grad = jnp.einsum(
        "td,te->de", attended_low, grad_branch, preferred_element_type=jnp.float32
    )
    grad_attended = jnp.einsum(
        "te,de->td", grad_branch, w_output, preferred_element_type=jnp.float32
    ).astype(jnp.bfloat16)
    delta = jnp.sum(
        (grad_attended.astype(jnp.float32) * attention_result).reshape(
            row_count, head_count, head_dim
        ),
        axis=-1,
    ).T
    grad_heads = grad_attended.reshape(row_count, head_count, head_dim)

    def block_grads(block_index):
        probabilities = jnp.exp(scores_at(block_index) - log_total[..., None])
        grad_probs = jnp.einsum(
            "qhd,khd->hqk", grad_heads, value_block(block_index), preferred_element_type=jnp.float32
        )
        grad_scores = (probabilities * (grad_probs - delta[..., None])).astype(jnp.bfloat16)
        return (probabilities, grad_scores)

    def query_update(state_pair, block_index, grad_scores):
        grad_query, table_grad = state_pair
        grad_query = grad_query + jnp.einsum(
            "hqk,khd->qhd", grad_scores, key_block(block_index), preferred_element_type=jnp.float32
        )
        table_grad = table_grad + table_terms(grad_scores, first_row, block_index * block_size)
        return (grad_query, table_grad)

    start_grads = (
        jnp.zeros((row_count, head_count, head_dim), jnp.float32),
        jnp.zeros((bucket_count, head_count), jnp.float32),
    )

    def backward_block(state_pair, block_index):
        probabilities, grad_scores = block_grads(block_index)
        new_state = query_update(state_pair, block_index, grad_scores)
        grad_value = jnp.einsum(
            "hqk,qhd->khd",
            probabilities.astype(jnp.bfloat16),
            grad_heads,
            preferred_element_type=jnp.float32,
        )
        grad_key = jnp.einsum(
            "hqk,qhd->khd", grad_scores, query_heads, preferred_element_type=jnp.float32
        )
        term = jnp.concatenate(
            (
                grad_key.reshape(block_size, model_width),
                grad_value.reshape(block_size, model_width),
            ),
            axis=1,
        )
        return (new_state, term)

    (grad_query, table_grad), key_terms = lax.scan(
        backward_block, start_grads, jnp.arange(block_count)
    )
    key_terms = key_terms.reshape(seq_length, 2 * model_width)
    key_value_grad = lax.psum_scatter(
        key_terms.astype(jnp.bfloat16), "context", scatter_dimension=0, tiled=True
    ).astype(jnp.float32)
    grad_key_low = key_value_grad[:, :model_width].astype(jnp.bfloat16)
    grad_value_low = key_value_grad[:, model_width:].astype(jnp.bfloat16)
    grad_query_low = grad_query.reshape(row_count, model_width).astype(jnp.bfloat16)
    query_grad = jnp.einsum("td,te->de", hidden, grad_query_low, preferred_element_type=jnp.float32)
    key_grad = jnp.einsum("td,te->de", hidden, grad_key_low, preferred_element_type=jnp.float32)
    value_grad = jnp.einsum("td,te->de", hidden, grad_value_low, preferred_element_type=jnp.float32)
    grad_hidden = jnp.einsum(
        "te,de->td", grad_query_low, w_query, preferred_element_type=jnp.float32
    )
    grad_hidden = grad_hidden + jnp.einsum(
        "te,de->td", grad_key_low, w_key, preferred_element_type=jnp.float32
    )
    grad_hidden = grad_hidden + jnp.einsum(
        "te,de->td", grad_value_low, w_value, preferred_element_type=jnp.float32
    )
    grad_inputs_norm, gain_one_grad = norm_one_back(grad_hidden)
    tokens_grad = (grad_middle + grad_inputs_norm).astype(jnp.bfloat16).reshape(tokens.shape)
    layer_out = layer_sum.astype(jnp.bfloat16).reshape(tokens.shape)
    shares = (
        lax.psum_scatter(
            gain_one_grad.astype(jnp.bfloat16), "fsdp", scatter_dimension=0, tiled=True
        ).astype(jnp.float32),
        lax.psum_scatter(
            query_grad.astype(jnp.bfloat16), "fsdp", scatter_dimension=0, tiled=True
        ).astype(jnp.float32),
        lax.psum_scatter(
            key_grad.astype(jnp.bfloat16), "fsdp", scatter_dimension=0, tiled=True
        ).astype(jnp.float32),
        lax.psum_scatter(
            value_grad.astype(jnp.bfloat16), "fsdp", scatter_dimension=0, tiled=True
        ).astype(jnp.float32),
        lax.psum_scatter(
            output_grad.astype(jnp.bfloat16), "fsdp", scatter_dimension=0, tiled=True
        ).astype(jnp.float32),
        lax.psum_scatter(
            table_grad.astype(jnp.bfloat16), "fsdp", scatter_dimension=0, tiled=True
        ).astype(jnp.float32),
        lax.psum_scatter(
            gain_two_grad.astype(jnp.bfloat16), "fsdp", scatter_dimension=0, tiled=True
        ).astype(jnp.float32),
        lax.psum_scatter(
            router_grad.astype(jnp.bfloat16), "fsdp", scatter_dimension=0, tiled=True
        ).astype(jnp.float32),
        lax.psum_scatter(
            first_grad.astype(jnp.bfloat16), "fsdp", scatter_dimension=1, tiled=True
        ).astype(jnp.float32),
        lax.psum_scatter(
            second_grad.astype(jnp.bfloat16), "fsdp", scatter_dimension=1, tiled=True
        ).astype(jnp.float32),
    )
    dense_part = lax.psum(
        (shares[0], shares[1], shares[2], shares[3], shares[4], shares[5], shares[6], shares[7]),
        ("context", "expert"),
    )
    expert_part = (
        lax.psum(shares[8].astype(jnp.bfloat16), "context").astype(jnp.float32),
        lax.psum(shares[9].astype(jnp.bfloat16), "context").astype(jnp.float32),
    )
    table_share = dense_part[5]
    return (
        layer_out,
        tokens_grad,
        dense_part[0],
        dense_part[1],
        dense_part[2],
        dense_part[3],
        dense_part[4],
        table_share,
        dense_part[6],
        dense_part[7],
        expert_part[0],
        expert_part[1],
    )


def solution(mesh):
    return jax.shard_map(
        per_device,
        mesh=mesh,
        in_specs=(
            P(("fsdp", "expert"), "context", None),
            P(("fsdp", "expert"), "context", None),
            P(("fsdp", "expert"), "context"),
            P(("fsdp", "expert"), "context"),
            P(),
            P("fsdp"),
            P("fsdp", None),
            P("fsdp", None),
            P("fsdp", None),
            P("fsdp", None),
            P("fsdp", None),
            P("fsdp"),
            P("fsdp", None),
            P("expert", "fsdp", None),
            P("expert", "fsdp", None),
        ),
        out_specs=(
            P(("fsdp", "expert"), "context", None),
            P(("fsdp", "expert"), "context", None),
            P("fsdp"),
            P("fsdp", None),
            P("fsdp", None),
            P("fsdp", None),
            P("fsdp", None),
            P("fsdp", None),
            P("fsdp"),
            P("fsdp", None),
            P("expert", "fsdp", None),
            P("expert", "fsdp", None),
        ),
        check_vma=False,
    )
```

profile of v0, /device:TPU:1, one launch (start us, length us, event | category | flops | bytes accessed | tf_op | source)
XLA Modules:
  0.0 1966.9 jit_solution(8894903695100854201)
XLA Ops:
  112.8 258.6 %while.51 = (s32[]{:T(128)}, f32[12,512]{1,0:T(8,128)S(1)}, f32[12,512]{1,0:T(8,128)S(1)}, s32[2]{0:T(128)S(1)}, bf16[1024,768]{0,1:T(8,128)(2,1)S(1)}, /*index=...) while((s32[]{:T(128)}, f32[12,512]{1,0:T(8,128)S(1)}, ...), condition=%wide.region_4.5_spmd.clone, body=%wide.region_1.4_spmd.clone.sunk | while | flops 424704000 | bytes 154472592 | solution.py:146
  121.1 35.3 %tile.58 = bf16[12,524799]{1,0:T(8,128)(2,1)} reshape(bf16[12,513,1023]{2,1,0:T(8,128)(2,1)} %tile.57) | data formatting | bytes 25190352 | tf_op jit(solution)/shard_map/while/body/eval_jaxpr/tile | solution.py:94
  171.8 37.2 %reshape.368 = bf16[12,512,1022]{2,1,0:T(8,128)(2,1)} reshape(bf16[12,523264]{1,0:T(8,128)(2,1)} %slice.106) | data formatting | bytes 25116672 | tf_op jit(solution)/shard_map/while/body/eval_jaxpr/reshape | solution.py:98
  250.1 34.9 %tile.58 = bf16[12,524799]{1,0:T(8,128)(2,1)} reshape(bf16[12,513,1023]{2,1,0:T(8,128)(2,1)} %tile.57) | data formatting | bytes 25190352 | tf_op jit(solution)/shard_map/while/body/eval_jaxpr/tile | solution.py:94
  300.2 37.2 %reshape.368 = bf16[12,512,1022]{2,1,0:T(8,128)(2,1)} reshape(bf16[12,523264]{1,0:T(8,128)(2,1)} %slice.106) | data formatting | bytes 25116672 | tf_op jit(solution)/shard_map/while/body/eval_jaxpr/reshape | solution.py:98
  374.1 253.7 %while.52 = (s32[]{:T(128)}, f32[512,12,64]{0,2,1:T(8,128)}, s32[2]{0:T(128)S(1)}, bf16[1024,768]{0,1:T(8,128)(2,1)}, bf16[1024,768]{0,1:T(8,128)(2,1)S(1)}, /*i...) while((s32[]{:T(128)}, f32[512,12,64]{0,2,1:T(8,128)}, ...), condition=%wide.region_6.7_spmd.clone, body=%wide.region_5.6_spmd.clone.sunk | while | flops 818675712 | bytes 128225416 | solution.py:159
  390.5 34.9 %tile.60 = bf16[12,524799]{1,0:T(8,128)(2,1)} reshape(bf16[12,513,1023]{2,1,0:T(8,128)(2,1)} %tile.59) | data formatting | bytes 25190352 | tf_op jit(solution)/shard_map/while/body/eval_jaxpr/tile | solution.py:94
  440.7 37.2 %reshape.369 = bf16[12,512,1022]{2,1,0:T(8,128)(2,1)} reshape(bf16[12,523264]{1,0:T(8,128)(2,1)} %slice.108) | data formatting | bytes 25116672 | tf_op jit(solution)/shard_map/while/body/eval_jaxpr/reshape | solution.py:98
  510.5 34.9 %tile.60 = bf16[12,524799]{1,0:T(8,128)(2,1)} reshape(bf16[12,513,1023]{2,1,0:T(8,128)(2,1)} %tile.59) | data formatting | bytes 25190352 | tf_op jit(solution)/shard_map/while/body/eval_jaxpr/tile | solution.py:94
  560.6 37.2 %reshape.369 = bf16[12,512,1022]{2,1,0:T(8,128)(2,1)} reshape(bf16[12,523264]{1,0:T(8,128)(2,1)} %slice.108) | data formatting | bytes 25116672 | tf_op jit(solution)/shard_map/while/body/eval_jaxpr/reshape | solution.py:98
  761.4 803.0 %while.53 = (s32[]{:T(128)}, f32[512,12,64]{0,2,1:T(8,128)}, f32[32,12]{0,1:T(8,128)}, bf16[2,512,1536]{2,1,0:T(8,128)(2,1)}, s32[2]{0:T(128)}, /*index=5*/bf16[...) while((s32[]{:T(128)}, f32[512,12,64]{0,2,1:T(8,128)}, ...), condition=%wide.region_16.17_spmd.clone, body=%wide.region_14.0_spmd.clone.sunk | while | flops 2059675904 | bytes 592682176 | solution.py:300
  779.8 35.1 %tile.62 = bf16[12,524799]{1,0:T(8,128)(2,1)} reshape(bf16[12,513,1023]{2,1,0:T(8,128)(2,1)} %tile.61) | data formatting | bytes 25190352 | tf_op jit(solution)/shard_map/while/body/eval_jaxpr/tile | solution.py:94
  830.1 37.2 %reshape.370 = bf16[12,512,1022]{2,1,0:T(8,128)(2,1)} reshape(bf16[12,523264]{1,0:T(8,128)(2,1)} %slice.110) | data formatting | bytes 25116672 | tf_op jit(solution)/shard_map/while/body/eval_jaxpr/reshape | solution.py:98
  910.9 95.1 %rev.11 = f32[12,512,512]{1,2,0:T(8,128)} reverse(bf16[12,512,512]{1,2,0:T(8,128)(2,1)} %copy-done), dimensions={1} | reverse | bytes 18874368 | tf_op jit(solution)/shard_map/while/body/eval_jaxpr/rev | solution.py:104
  1044.1 39.7 %copy.162 = f32[2,8,512,1024]{3,1,2,0:T(8,128)} copy(f32[2,8,512,1024]{3,2,1,0:T(8,128)S(1)} %bitcast.355) | data formatting | bytes 67108864 | tf_op jit(solution)/shard_map/while
  1106.3 41.4 %reshape.371 = f32[12,512,1023]{2,1,0:T(8,128)} reshape(f32[12,523776]{1,0:T(8,128)} %slice.112) | data formatting | bytes 50282496 | tf_op jit(solution)/shard_map/while/body/eval_jaxpr/reshape | solution.py:109
  1176.9 35.0 %tile.62 = bf16[12,524799]{1,0:T(8,128)(2,1)} reshape(bf16[12,513,1023]{2,1,0:T(8,128)(2,1)} %tile.61) | data formatting | bytes 25190352 | tf_op jit(solution)/shard_map/while/body/eval_jaxpr/tile | solution.py:94
  1227.2 37.2 %reshape.370 = bf16[12,512,1022]{2,1,0:T(8,128)(2,1)} reshape(bf16[12,523264]{1,0:T(8,128)(2,1)} %slice.110) | data formatting | bytes 25116672 | tf_op jit(solution)/shard_map/while/body/eval_jaxpr/reshape | solution.py:98
  1308.4 95.1 %rev.11 = f32[12,512,512]{1,2,0:T(8,128)} reverse(bf16[12,512,512]{1,2,0:T(8,128)(2,1)} %copy-done), dimensions={1} | reverse | bytes 18874368 | tf_op jit(solution)/shard_map/while/body/eval_jaxpr/rev | solution.py:104
  1441.5 39.7 %copy.162 = f32[2,8,512,1024]{3,1,2,0:T(8,128)} copy(f32[2,8,512,1024]{3,2,1,0:T(8,128)S(1)} %bitcast.355) | data formatting | bytes 67108864 | tf_op jit(solution)/shard_map/while
  1503.8 41.4 %reshape.371 = f32[12,512,1023]{2,1,0:T(8,128)} reshape(f32[12,523776]{1,0:T(8,128)} %slice.112) | data formatting | bytes 50282496 | tf_op jit(solution)/shard_map/while/body/eval_jaxpr/reshape | solution.py:109
  1599.9 36.7 %reduce-scatter.21.cloned.1.call-done = bf16[1,192,3072]{2,1,0:T(8,128)(2,1)} async-done(((bf16[1,768,3072]{2,1,0:T(8,128)(2,1)}), bf16[1,192,3072]{2,1,0:T(8,128)(2,1)}) %reduce-scatter.21.cloned.1.call-update) | async-done | bytes 1179664 | tf_op jit(solution)/shard_map/reduce_scatter | solution.py:350
  1636.6 60.4 %reduce-scatter.23.cloned.1.call-done = bf16[1,768,768]{2,1,0:T(8,128)(2,1)} async-done(((bf16[1,3072,768]{2,1,0:T(8,128)(2,1)}), bf16[1,768,768]{2,1,0:T(8,128)(2,1)}) %reduce-scatter.23.cloned.1.call-update) | async-done | bytes 1179664 | tf_op jit(solution)/shard_map/reduce_scatter | solution.py:353
  1851.7 103.8 %all-reduce.14 = (f32[192]{0:T(256)}, f32[192,768]{1,0:T(8,128)}, f32[192,768]{1,0:T(8,128)}, f32[192,768]{1,0:T(8,128)}, f32[192,768]{1,0:T(8,128)}, /*index=5*...) all-reduce(f32[192]{0:T(256)S(1)} %get-tuple-element.1017, ...), channel_id=1, replica_groups=mesh['fsdp'=4,'context'=2,'expert'=4] {'context','expert'}, use_global_device_ids=true, to_apply=%region_21.22 | all-reduce | flops 591072 | bytes 3547392 | tf_op jit(solution)/shard_map/psum | solution.py:357
  (356 shorter events, 933.9 us)
Async XLA Ops:
  7.2 32.5 %all-gather.14.cloned.1.call-start = ((), (), s32[]{:S(2)}) async-start(), calls=%async_computation.14 | async-start | bytes 1474560 | tf_op jit(solution)/shard_map/all_gather | solution.py:58
  7.9 61.4 %all-gather.10.cloned.1.call-start = ((), (), s32[]{:S(2)}) async-start(), calls=%async_computation.12 | async-start | bytes 1474560 | tf_op jit(solution)/shard_map/all_gather | solution.py:59
  8.7 90.3 %all-gather.18.cloned.1.call-start = ((), (), s32[]{:S(2)}) async-start(), calls=%async_computation.16 | async-start | bytes 1474560 | tf_op jit(solution)/shard_map/all_gather | solution.py:57
  9.4 101.7 %all-gather.16.cloned.1.call-start = ((), (), s32[]{:S(2)}) async-start(), calls=%async_computation.15 | async-start | bytes 2359296 | tf_op jit(solution)/shard_map/all_gather | solution.py:76
  42.7 328.8 %all-gather.12.cloned.1.call-start = ((), (), s32[]{:S(2)}) async-start(), calls=%async_computation.13 | async-start | bytes 2359296 | tf_op jit(solution)/shard_map/all_gather | solution.py:77
  72.3 555.5 %all-gather.20.cloned.1.call-start = ((), (), s32[]{:S(2)}) async-start(), calls=%async_computation.17 | async-start | bytes 1474560 | tf_op jit(solution)/shard_map/all_gather | solution.py:60
  72.9 593.5 %all-gather.22.cloned.1.call-start = ((), (), s32[]{:S(2)}) async-start(), calls=%async_computation.18 | async-start | bytes 5898240 | tf_op jit(solution)/shard_map/all_gather | solution.py:64
  73.6 601.7 %all-gather.24.cloned.1.call-start = ((), (), s32[]{:S(2)}) async-start(), calls=%async_computation.19 | async-start | bytes 5898240 | tf_op jit(solution)/shard_map/all_gather | solution.py:65
  633.3 28.8 %all-to-all-start = ((bf16[4,1,160,768]{3,2,1,0:T(8,128)(2,1)}), bf16[4,1,160,768]{3,2,1,0:T(8,128)(2,1)}, u32[]{:S(2)}, u32[]{:S(2)}) async-start(bf16[4,1,160,768]{3,2,1,0:T(8,128)(2,1)} %bitcast.372), calls=%async_computation | async-start | bytes 1966080 | tf_op jit(solution)/shard_map/all_to_all | solution.py:186
  645.3 105.6 %copy-start.36 = (f32[512]{0:T(512)}, f32[512]{0:T(512)S(1)}, u32[]{:S(2)}) copy-start(f32[512]{0:T(512)S(1)} %get-tuple-element.994) | copy-start | bytes 6148
  662.1 28.1 %all-to-all-start.2 = ((bf16[4,1,160,768]{3,2,1,0:T(8,128)(2,1)}), bf16[4,1,160,768]{3,2,1,0:T(8,128)(2,1)}, u32[]{:S(2)}, u32[]{:S(2)}) async-start(bf16[4,1,160,768]{3,2,1,0:T(8,128)(2,1)} %bitcast.373), calls=%async_computation.2 | async-start | bytes 1966080 | tf_op jit(solution)/shard_map/all_to_all | solution.py:209
  690.2 28.5 %all-to-all-start.1 = ((bf16[4,1,160,768]{3,2,1,0:T(8,128)(2,1)}), bf16[4,1,160,768]{3,2,1,0:T(8,128)(2,1)}, u32[]{:S(2)}, u32[]{:S(2)}) async-start(bf16[4,1,160,768]{3,2,1,0:T(8,128)(2,1)} %fusion.77), calls=%async_computation.1 | async-start | bytes 1966080 | tf_op jit(solution)/shard_map/all_to_all | solution.py:192
  718.8 28.1 %all-to-all-start.3 = ((bf16[4,1,160,768]{3,2,1,0:T(8,128)(2,1)}), bf16[4,1,160,768]{3,2,1,0:T(8,128)(2,1)}, u32[]{:S(2)}, u32[]{:S(2)}) async-start(bf16[4,1,160,768]{3,2,1,0:T(8,128)(2,1)} %fusion.82), calls=%async_computation.3 | async-start | bytes 1966080 | tf_op jit(solution)/shard_map/all_to_all | solution.py:227
  723.0 870.4 %reduce-scatter.11.cloned.1.call-start = ((), (), s32[]{:S(2)}) async-start(), calls=%async_computation.20 | async-start | bytes 4718592 | tf_op jit(solution)/shard_map/reduce_scatter | solution.py:304
  1564.3 72.3 %reduce-scatter.21.cloned.1.call-start = ((), (), s32[]{:S(2)}) async-start(), calls=%async_computation.25 | async-start | bytes 5898240 | tf_op jit(solution)/shard_map/reduce_scatter | solution.py:350
  1572.9 124.1 %reduce-scatter.23.cloned.1.call-start = ((), (), s32[]{:S(2)}) async-start(), calls=%async_computation.26 | async-start | bytes 5898240 | tf_op jit(solution)/shard_map/reduce_scatter | solution.py:353
  1584.0 139.9 %reduce-scatter.25.cloned.1.call-start = ((), (), s32[]{:S(2)}) async-start(), calls=%async_computation.27 | async-start | bytes 245760
  1586.4 169.8 %reduce-scatter.19.cloned.1.call-start = ((), (), s32[]{:S(2)}) async-start(), calls=%async_computation.24 | async-start | bytes 1474560 | tf_op jit(solution)/shard_map/reduce_scatter | solution.py:338
  1589.9 198.4 %reduce-scatter.13.cloned.1.call-start = ((), (), s32[]{:S(2)}) async-start(), calls=%async_computation.21 | async-start | bytes 1474560 | tf_op jit(solution)/shard_map/reduce_scatter | solution.py:329
  1593.3 226.7 %reduce-scatter.17.cloned.1.call-start = ((), (), s32[]{:S(2)}) async-start(), calls=%async_computation.23 | async-start | bytes 1474560 | tf_op jit(solution)/shard_map/reduce_scatter | solution.py:335
  1596.5 255.2 %reduce-scatter.15.cloned.1.call-start = ((), (), s32[]{:S(2)}) async-start(), calls=%async_computation.22 | async-start | bytes 1474560 | tf_op jit(solution)/shard_map/reduce_scatter | solution.py:332
  1599.8 98.5 %copy-start.52 = (f32[32,12]{0,1:T(8,128)S(1)}, f32[32,12]{0,1:T(8,128)}, u32[]{:S(2)}) copy-start(f32[32,12]{0,1:T(8,128)} %get-tuple-element.653) | copy-start | bytes 4612
  1599.8 98.6 %copy-start.26 = (bf16[512,12,64]{0,2,1:T(8,128)(2,1)S(1)}, bf16[512,12,64]{0,2,1:T(8,128)(2,1)}, u32[]{:S(2)}) copy-start(bf16[512,12,64]{0,2,1:T(8,128)(2,1)} %copy-done.25) | copy-start | bytes 2359300
  1599.9 355.6 %all-reduce.13.cloned.1.call-start = ((), (), s32[]{:S(2)}) async-start(), calls=%async_computation.28 | async-start | bytes 4718592 | tf_op jit(solution)/shard_map/psum | solution.py:362
  (66 other events, 673.5 us)
Sparse Core Ops, SparseCore 0:
  9.9 29.7 all-gather.13
  41.5 27.7 all-gather.9
  71.1 27.7 all-gather.17
  100.9 10.1 all-gather.15
  113.1 10.9 all-gather.11
  125.8 28.5 all-gather.19
  156.2 57.0 all-gather.21
  215.1 57.0 all-gather.23
  1564.5 11.0 reduce-scatter.10
  1578.7 57.9 reduce-scatter.20
  1639.9 57.0 reduce-scatter.22
  1700.4 23.5 reduce-scatter.24
  1727.1 29.0 reduce-scatter.18
  1759.8 28.5 reduce-scatter.12
  1791.4 28.6 reduce-scatter.16
  1823.1 28.5 reduce-scatter.14
  1854.0 22.0 all-reduce.12
where the time goes:
time: 2000 us; the launch traced here: 1970 us
  local copies, waits for them, and re-layouts  1170 us (58%)
  waiting for transfers between devices  337 us (17%)
  matrix products  205 us (10%)
  blocking collectives  137 us (7%)
  other arithmetic  51.2 us (3%)
  loops' own time  29.9 us (1%)
    another operation x12, local copies, waits for them, and re-layouts, bias_block(): repeated = jnp.tile(window, (1, query_count + 1))  248 us
    reshape x6, local copies, waits for them, and re-layouts, bias_block(): return skewed.reshape(head_count, query_count, width - 1)[:, :, :key_count]  223 us
    rev x2, local copies, waits for them, and re-layouts, table_terms(): flipped = grad_scores.astype(jnp.float32)[:, ::-1, :]  190 us
    while x62, local copies, waits for them, and re-layouts  181 us
    psum x1, blocking collectives, per_device(): lax.psum((shares[0], shares[1], shares[2], shares[3], shares[4], shares[5...  104 us
    slice x6, local copies, waits for them, and re-layouts, bias_block(): lax.slice_in_dim(repeated, query_count - 1, query_count - 1 + query_count...  92.1 us
    reshape x2, local copies, waits for them, and re-layouts, table_terms(): flat.reshape(head_count, query_count, width)  82.8 us
    reduce_scatter x1, waiting for transfers between devices, per_device(): lax.psum_scatter(second_grad.astype(jnp.bfloat16), 'fsdp', scatter_dimens...  60.4 us
  transfers between devices with their start and end apart: 21, of which 15 were waited for; matrix products, arithmetic and copies ran while one was open for 31% of the time, Pallas kernels for 0%

commit v1 on v0

v1 whole, which is shorter than its diff:
```python
import functools

import jax
import jax.numpy as jnp
from jax import lax
from jax.experimental import pallas as pl
from jax.experimental.pallas import tpu as pltpu
from jax.sharding import PartitionSpec as P

highest_score = lax.Precision.HIGHEST
epsilon = 1e-06
low = jnp.bfloat16
full = jnp.float32
lane_count = 128


def dot_over(left, right, left_dim, right_dim):
    return lax.dot_general(
        left, right, (((left_dim,), (right_dim,)), ((), ())), preferred_element_type=full
    )


def bias_strip(window):
    width = window.shape[1]
    spread = jnp.broadcast_to(window, (lane_count, width))
    rolled = pltpu.roll(spread, width - lane_count + 1, 1, stride=1, stride_axis=0)
    return rolled[:, : width - lane_count].T


def attention_forward(width, query_ref, key_ref, value_ref, window_ref, out_ref, log_ref, strip_ref):
    queries = query_ref.shape[0]
    keys = key_ref.shape[0]
    per_step = lane_count // width
    tiles = queries // lane_count
    lanes = lax.broadcasted_iota(jnp.int32, (1, lane_count), 1) // width
    rows = lax.broadcasted_iota(jnp.int32, (lane_count, 1), 0) // width
    values_turned = value_ref[...].T
    for head in range(per_step):
        strip_ref[head] = bias_strip(window_ref[head])
    for tile in range(tiles):
        span = pl.ds(tile * lane_count, lane_count)
        query_tile = query_ref[span, :]
        total = jnp.zeros((lane_count, lane_count), full)
        for head in range(per_step):
            own = jnp.where(lanes == head, query_tile, jnp.zeros_like(query_tile))
            scores = dot_over(key_ref[...], own, 1, 1)
            scores = scores + strip_ref[head, pl.ds((tiles - 1 - tile) * lane_count, keys), :]
            top = jnp.max(scores, axis=0, keepdims=True)
            raised = jnp.exp(scores - top)
            summed = jnp.sum(raised, axis=0, keepdims=True)
            log_ref[head, :, span] = top + jnp.log(summed)
            part = dot_over(values_turned, raised.astype(low), 1, 0) / summed
            total = jnp.where(rows == head, part, total)
        out_ref[span, :] = total.T.astype(low)


def diagonal_fold(strip_sum, window_width):
    turned = strip_sum.T
    turned = jnp.concatenate(
        (turned, jnp.zeros((lane_count, window_width - turned.shape[1]), full)), axis=1
    )
    size = lane_count
    while size > 1:
        size //= 2
        turned = pltpu.roll(turned[:size], size, 1) + turned[size : 2 * size]
    return turned


def attention_backward(
    width,
    query_ref,
    key_ref,
    value_ref,
    grad_ref,
    log_ref,
    window_ref,
    query_grad_ref,
    key_grad_ref,
    value_grad_ref,
    diagonal_ref,
    strip_ref,
    sums_ref,
    key_total,
    value_total,
):
    queries = query_ref.shape[0]
    keys = key_ref.shape[0]
    per_step = lane_count // width
    tiles = queries // lane_count
    lanes = lax.broadcasted_iota(jnp.int32, (1, lane_count), 1) // width
    rows = lax.broadcasted_iota(jnp.int32, (lane_count, 1), 0) // width
    keys_turned = key_ref[...].T
    for head in range(per_step):
        strip_ref[head] = bias_strip(window_ref[head])
    sums_ref[...] = jnp.zeros_like(sums_ref)
    key_total[...] = jnp.zeros_like(key_total)
    value_total[...] = jnp.zeros_like(value_total)
    for tile in range(tiles):
        span = pl.ds(tile * lane_count, lane_count)
        shifted = pl.ds((tiles - 1 - tile) * lane_count, keys)
        query_tile = query_ref[span, :]
        grad_tile = grad_ref[span, :]
        total = jnp.zeros((lane_count, lane_count), full)
        for head in range(per_step):
            own_query = jnp.where(lanes == head, query_tile, jnp.zeros_like(query_tile))
            own_grad = jnp.where(lanes == head, grad_tile, jnp.zeros_like(grad_tile))
            scores = dot_over(key_ref[...], own_query, 1, 1) + strip_ref[head, shifted, :]
            probs = jnp.exp(scores - log_ref[head, :, span])
            grad_probs = dot_over(value_ref[...], own_grad, 1, 1)
            weighted = probs * grad_probs
            delta = jnp.sum(weighted, axis=0, keepdims=True)
            grad_scores = (weighted - probs * delta).astype(low)
            sums_ref[head, shifted, :] += grad_scores.astype(full)
            value_total[...] += dot_over(probs.astype(low), own_grad, 1, 0)
            key_total[...] += dot_over(grad_scores, own_query, 1, 0)
            part = dot_over(keys_turned, grad_scores, 1, 0)
            total = jnp.where(rows == head, part, total)
        query_grad_ref[span, :] = total.T.astype(low)
    key_grad_ref[...] = key_total[...].astype(low)
    value_grad_ref[...] = value_total[...].astype(low)
    for head in range(per_step):
        diagonal_ref[head] = diagonal_fold(sums_ref[head], diagonal_ref.shape[2])


def forward_call(query_rows, keys_all, values_all, windows):
    queries, model_width = query_rows.shape
    keys = keys_all.shape[0]
    heads, _, span = windows.shape
    width = model_width // heads
    per_step = lane_count // width
    row_block = pl.BlockSpec((queries, lane_count), lambda h: (0, h))
    key_block = pl.BlockSpec((keys, lane_count), lambda h: (0, h))
    return pl.pallas_call(
        functools.partial(attention_forward, width),
        grid=(heads // per_step,),
        in_specs=[
            row_block,
            key_block,
            key_block,
            pl.BlockSpec((per_step, 1, span), lambda h: (h, 0, 0)),
        ],
        out_specs=[row_block, pl.BlockSpec((per_step, 1, queries), lambda h: (h, 0, 0))],
        out_shape=[
            jax.ShapeDtypeStruct((queries, model_width), low),
            jax.ShapeDtypeStruct((heads, 1, queries), full),
        ],
        scratch_shapes=[pltpu.VMEM((per_step, span - lane_count, lane_count), full)],
        compiler_params=pltpu.CompilerParams(vmem_limit_bytes=40 * 2**20),
        name="attention_forward",
    )(query_rows, keys_all, values_all, windows)


def backward_call(query_rows, keys_all, values_all, grad_rows, logs, windows):
    queries, model_width = query_rows.shape
    keys = keys_all.shape[0]
    heads, _, span = windows.shape
    width = model_width // heads
    per_step = lane_count // width
    row_block = pl.BlockSpec((queries, lane_count), lambda h: (0, h))
    key_block = pl.BlockSpec((keys, lane_count), lambda h: (0, h))
    window_block = pl.BlockSpec((per_step, 1, span), lambda h: (h, 0, 0))
    return pl.pallas_call(
        functools.partial(attention_backward, width),
        grid=(heads // per_step,),
        in_specs=[
            row_block,
            key_block,
            key_block,
            row_block,
            pl.BlockSpec((per_step, 1, queries), lambda h: (h, 0, 0)),
            window_block,
        ],
        out_specs=[row_block, key_block, key_block, window_block],
        out_shape=[
            jax.ShapeDtypeStruct((queries, model_width), low),
            jax.ShapeDtypeStruct((keys, model_width), low),
            jax.ShapeDtypeStruct((keys, model_width), low),
            jax.ShapeDtypeStruct((heads, 1, span), full),
        ],
        scratch_shapes=[
            pltpu.VMEM((per_step, span - lane_count, lane_count), full),
            pltpu.VMEM((per_step, span - lane_count, lane_count), full),
            pltpu.VMEM((keys, lane_count), full),
            pltpu.VMEM((keys, lane_count), full),
        ],
        compiler_params=pltpu.CompilerParams(vmem_limit_bytes=40 * 2**20),
        name="attention_backward",
    )(query_rows, keys_all, values_all, grad_rows, logs, windows)


def swap(values, axis, distance):
    size = lax.axis_size(axis)
    return lax.ppermute(values, axis, [(place, place ^ distance) for place in range(size)])


def paired():
    return lax.axis_size("context") == 2


def square_gather(piece):
    half = piece.shape[-1] // 2
    one = swap(piece, "fsdp", 1)
    two = swap(piece, "fsdp", 2)
    far = jnp.concatenate(
        (swap(two[..., :half], "fsdp", 1), swap(one[..., half:], "fsdp", 2)), axis=-1
    )
    return (piece, one, two, far)


def place_pieces(pieces, start, place):
    for distance, piece in enumerate(pieces):
        start = place(start, piece, lax.axis_index("fsdp") ^ distance)
    return start


def gather_rows(shard):
    if lax.axis_size("fsdp") != 4:
        return lax.all_gather(shard, "fsdp", axis=0, tiled=True)
    rows, columns = shard.shape
    if not paired():
        return place_pieces(
            square_gather(shard),
            jnp.zeros((4, rows, columns), shard.dtype),
            lambda whole, piece, owner: lax.dynamic_update_slice(whole, piece[None], (owner, 0, 0)),
        ).reshape(4 * rows, columns)
    core = lax.axis_index("context")
    half = rows // 2
    mine = square_gather(lax.dynamic_slice_in_dim(shard, core * half, half, 0))
    theirs = [swap(piece, "context", 1) for piece in mine]
    whole = jnp.zeros((4, 2, half, columns), shard.dtype)

    def place_at(side):
        return lambda whole, piece, owner: lax.dynamic_update_slice(
            whole, piece[None, None], (owner, side, 0, 0)
        )

    whole = place_pieces(mine, whole, place_at(core))
    whole = place_pieces(theirs, whole, place_at(1 - core))
    return whole.reshape(4 * rows, columns)


def gather_flat(vector):
    if lax.axis_size("fsdp") != 4:
        return lax.all_gather(vector, "fsdp", axis=0)
    row = lax.axis_index("fsdp")
    near = swap(vector, "fsdp", 1)
    pair = jnp.stack((vector, near))
    other = swap(pair, "fsdp", 2)
    whole = jnp.zeros((4,) + vector.shape, vector.dtype)
    for distance, piece in enumerate((pair[0], pair[1], other[0], other[1])):
        whole = lax.dynamic_update_slice(whole, piece[None], (row ^ distance, 0))
    return whole


def take(blocks, place):
    return lax.dynamic_index_in_dim(blocks, place, 0, keepdims=False)


def add_low(left, right):
    return (left.astype(full) + right.astype(full)).astype(low)


def square_scatter(blocks):
    row = lax.axis_index("fsdp")
    half = blocks.shape[-1] // 2
    results = []
    for part, (first, second) in ((blocks[..., :half], (1, 2)), (blocks[..., half:], (2, 1))):
        away = jnp.stack((take(part, row ^ first), take(part, row ^ 3)))
        came = swap(away, "fsdp", first)
        onward = add_low(take(part, row ^ second), came[1])
        kept = take(part, row).astype(full) + came[0].astype(full)
        results.append(kept + swap(onward, "fsdp", second).astype(full))
    return jnp.concatenate(results, axis=-1)


def scatter_half(grad):
    rows, columns = grad.shape
    core = lax.axis_index("context")
    blocks = grad.astype(low).reshape(4, 2, rows // 8, columns)

    def side(which):
        return lax.dynamic_index_in_dim(blocks, which, 1, keepdims=False)

    came = swap(side(1 - core), "context", 1)
    return square_scatter(add_low(side(core), came))


def join_cores(half):
    core = lax.axis_index("context")
    other = swap(half, "context", 1)
    whole = jnp.zeros((2,) + half.shape, half.dtype)
    whole = lax.dynamic_update_slice(whole, half[None], (core, 0, 0))
    whole = lax.dynamic_update_slice(whole, other[None], (1 - core, 0, 0))
    return whole.reshape(2 * half.shape[0], half.shape[1]).astype(full)


def sum_experts(share):
    size = lax.axis_size("expert")
    rows, columns = share.shape
    if size != 4 or rows % 64:
        return lax.psum(share, "expert")
    row = lax.axis_index("expert")
    blocks = share.astype(low).reshape(4, rows // 4, columns)
    own = take(blocks, row).astype(full)
    for distance in (1, 2, 3):
        own = own + swap(take(blocks, row ^ distance), "expert", distance).astype(full)
    own = own.astype(low)
    whole = lax.dynamic_update_slice(jnp.zeros_like(blocks), own[None], (row, 0, 0))
    for distance in (1, 2, 3):
        came = swap(own, "expert", distance)
        whole = lax.dynamic_update_slice(whole, came[None], (row ^ distance, 0, 0))
    return whole.reshape(rows, columns)


def dense_reduce(grad):
    if lax.axis_size("fsdp") == 4 and paired():
        half = scatter_half(grad)
        tall = half.reshape(-1, 768 if half.size % 768 == 0 else half.shape[1])
        return join_cores(sum_experts(tall).reshape(half.shape).astype(low))
    share = lax.psum_scatter(grad.astype(low), "fsdp", scatter_dimension=0, tiled=True)
    return lax.psum(share.astype(full), ("context", "expert"))


def expert_reduce(grad):
    if lax.axis_size("fsdp") == 4 and paired():
        return join_cores(scatter_half(grad).astype(low))
    share = lax.psum_scatter(grad.astype(low), "fsdp", scatter_dimension=0, tiled=True)
    return lax.psum(share, "context").astype(full)


def gather_positions(rows):
    if not paired():
        return lax.all_gather(rows, "context", axis=0, tiled=True)
    core = lax.axis_index("context")
    other = swap(rows, "context", 1)
    count = rows.shape[0]
    whole = jnp.zeros((2 * count,) + rows.shape[1:], rows.dtype)
    whole = lax.dynamic_update_slice(whole, rows, (core * count, 0))
    return lax.dynamic_update_slice(whole, other, ((1 - core) * count, 0))


def scatter_positions(rows):
    if not paired():
        return lax.psum_scatter(rows, "context", scatter_dimension=0, tiled=True)
    core = lax.axis_index("context")
    count = rows.shape[0] // 2
    came = swap(lax.dynamic_slice_in_dim(rows, (1 - core) * count, count, 0), "context", 1)
    return add_low(lax.dynamic_slice_in_dim(rows, core * count, count, 0), came)


def rms_norm(values, norm_gain):
    return (
        values * lax.rsqrt(jnp.mean(values * values, axis=-1, keepdims=True) + epsilon) * norm_gain
    )


def smooth(values):
    return jax.nn.gelu(values, approximate=True)


def per_device(
    tokens,
    cotangent,
    expert_ids,
    capacity_slot,
    buckets,
    attn_gain,
    query_weight,
    key_weight,
    value_weight,
    attention_output_matrix,
    bias_table,
    mixture_gain,
    router_matrix,
    expert_in,
    expert_out,
):
    row_count = tokens.shape[1]
    model_width = tokens.shape[2]
    inputs = tokens.reshape(row_count, model_width).astype(jnp.float32)
    upstream = cotangent.reshape(row_count, model_width).astype(jnp.float32)
    chosen = expert_ids.reshape(row_count)
    slot_ids = capacity_slot.reshape(row_count)
    seq_length = (buckets.shape[0] + 1) // 2
    gain_rows = attn_gain.shape[0]
    experts = router_matrix.shape[1]
    small = gather_flat(
        jnp.concatenate(
            (attn_gain, mixture_gain, router_matrix.reshape(-1), bias_table.reshape(-1))
        )
    )
    gain_one = small[:, :gain_rows].reshape(-1)
    gain_two = small[:, gain_rows : 2 * gain_rows].reshape(-1)
    w_router = small[:, 2 * gain_rows : (2 + experts) * gain_rows].reshape(-1, experts)
    table_rows = small[:, (2 + experts) * gain_rows :].reshape(-1, bias_table.shape[1])
    w_inner = gather_rows(jnp.concatenate((query_weight, key_weight, value_weight), axis=1))
    w_output = gather_rows(attention_output_matrix)
    w_first = gather_rows(expert_in[0])
    w_second = gather_rows(expert_out[0])
    head_count = table_rows.shape[1]
    head_dim = model_width // head_count
    bucket_count = table_rows.shape[0]
    normalized_input, norm_one_back = jax.vjp(rms_norm, inputs, gain_one.astype(jnp.float32))
    hidden = normalized_input.astype(jnp.bfloat16)
    inner = jnp.dot(hidden, w_inner, preferred_element_type=jnp.float32).astype(jnp.bfloat16)
    query_rows = inner[:, :model_width]
    pairs_all = gather_positions(inner[:, model_width:])
    keys_all = pairs_all[:, :model_width]
    values_all = pairs_all[:, model_width:]
    first_row = lax.axis_index("context") * row_count
    bucket_ids = jnp.arange(bucket_count, dtype=jnp.int32)
    window_start = seq_length - row_count - first_row
    window_buckets = lax.dynamic_slice_in_dim(
        jnp.pad(buckets, (0, 1)), window_start, row_count + seq_length, 0
    )
    offset_onehot = (window_buckets[:, None] == bucket_ids).astype(jnp.float32)
    windows = jnp.einsum(
        "ob,bh->ho", offset_onehot, table_rows.astype(jnp.float32), precision=highest_score
    )[:, None, :]
    attended_low, log_total = forward_call(query_rows, keys_all, values_all, windows)
    middle = inputs + jnp.dot(attended_low, w_output, preferred_element_type=jnp.float32)
    expert_groups = lax.axis_size("expert")
    capacity = row_count * 5 // (4 * experts)
    normed_two, norm_two_back = jax.vjp(rms_norm, middle, gain_two.astype(jnp.float32))
    second_hidden = normed_two.astype(jnp.bfloat16)
    router_logits = jnp.dot(second_hidden, w_router, preferred_element_type=jnp.float32)
    shifted = router_logits - jnp.max(router_logits, axis=-1, keepdims=True)
    raised = jnp.exp(shifted)
    router_probs = raised / jnp.sum(raised, axis=-1, keepdims=True)
    selector = (chosen[:, None] == jnp.arange(experts, dtype=jnp.int32)).astype(jnp.float32)
    gate_value = jnp.sum(router_probs * selector, axis=-1)
    position = chosen * capacity + slot_ids
    dispatch = (
        (position[:, None] == jnp.arange(experts * capacity, dtype=jnp.int32))
        & (slot_ids[:, None] >= 0)
    ).astype(jnp.bfloat16)
    outgoing = jnp.einsum("tc,td->cd", dispatch, second_hidden, preferred_element_type=jnp.float32)
    outgoing = outgoing.astype(jnp.bfloat16).reshape(
        expert_groups, capacity, model_width
    )
    received = lax.all_to_all(outgoing, "expert", split_axis=0, concat_axis=0, tiled=True)
    pre_act = jnp.einsum("scd,df->scf", received, w_first, preferred_element_type=jnp.float32)
    activated = smooth(pre_act).astype(jnp.bfloat16)
    produced = jnp.einsum(
        "scf,fd->scd", activated, w_second, preferred_element_type=jnp.float32
    ).astype(jnp.bfloat16)
    returned = lax.all_to_all(produced, "expert", split_axis=0, concat_axis=0, tiled=True)
    combined = jnp.einsum(
        "tc,cd->td",
        dispatch,
        returned.reshape(experts * capacity, model_width),
        preferred_element_type=jnp.float32,
    )
    layer_sum = middle + gate_value[:, None] * combined
    grad_gate = jnp.sum(upstream * combined, axis=-1)
    weighted_grad = (gate_value[:, None] * upstream).astype(jnp.bfloat16)
    grad_slots = jnp.einsum(
        "tc,td->cd", dispatch, weighted_grad, preferred_element_type=jnp.float32
    )
    grad_slots = grad_slots.astype(jnp.bfloat16).reshape(
        expert_groups, capacity, model_width
    )
    grad_produced = lax.all_to_all(grad_slots, "expert", split_axis=0, concat_axis=0, tiled=True)
    grad_act = jnp.einsum(
        "scd,fd->scf", grad_produced, w_second, preferred_element_type=jnp.float32
    )
    activated_again, smooth_back = jax.vjp(smooth, pre_act)
    grad_pre = smooth_back(grad_act)[0].astype(jnp.bfloat16)
    second_grad = jnp.einsum(
        "scf,scd->fd",
        activated_again.astype(jnp.bfloat16),
        grad_produced,
        preferred_element_type=jnp.float32,
    )
    first_grad = jnp.einsum(
        "scd,scf->df", received, grad_pre, preferred_element_type=jnp.float32
    )
    grad_received = jnp.einsum(
        "scf,df->scd", grad_pre, w_first, preferred_element_type=jnp.float32
    ).astype(jnp.bfloat16)
    grad_sent = lax.all_to_all(grad_received, "expert", split_axis=0, concat_axis=0, tiled=True)
    grad_hidden_two = jnp.einsum(
        "tc,cd->td",
        dispatch,
        grad_sent.reshape(experts * capacity, model_width),
        preferred_element_type=jnp.float32,
    )
    grad_logits = router_probs * (selector - gate_value[:, None]) * grad_gate[:, None]
    router_grad = jnp.einsum(
        "td,te->de", second_hidden.astype(jnp.float32), grad_logits, precision=highest_score
    )
    grad_hidden_two = grad_hidden_two + jnp.einsum(
        "te,de->td", grad_logits, w_router.astype(jnp.float32), precision=highest_score
    )
    grad_middle_norm, gain_two_grad = norm_two_back(grad_hidden_two)
    grad_middle = upstream + grad_middle_norm
    grad_branch = grad_middle.astype(jnp.bfloat16)
    output_grad = jnp.einsum(
        "td,te->de", attended_low, grad_branch, preferred_element_type=jnp.float32
    )
    grad_attended = jnp.einsum(
        "te,de->td", grad_branch, w_output, preferred_element_type=jnp.float32
    ).astype(jnp.bfloat16)
    grad_query_low, key_terms, value_terms, diagonals = backward_call(
        query_rows, keys_all, values_all, grad_attended, log_total, windows
    )
    table_grad = jnp.einsum(
        "hw,wb->bh", diagonals[:, 0, :], offset_onehot, precision=highest_score
    )
    pair_grad = scatter_positions(jnp.concatenate((key_terms, value_terms), axis=1))
    inner_grad = jnp.concatenate((grad_query_low, pair_grad), axis=1)
    inner_share = dense_reduce(
        jnp.einsum("td,te->de", hidden, inner_grad, preferred_element_type=jnp.float32)
    )
    grad_hidden = jnp.einsum("te,de->td", inner_grad, w_inner, preferred_element_type=jnp.float32)
    grad_inputs_norm, gain_one_grad = norm_one_back(grad_hidden)
    tokens_grad = (grad_middle + grad_inputs_norm).astype(jnp.bfloat16).reshape(tokens.shape)
    layer_out = layer_sum.astype(jnp.bfloat16).reshape(tokens.shape)
    fsdp_size = lax.axis_size("fsdp")
    small_sum = lax.psum(
        jnp.concatenate(
            [
                term.reshape(fsdp_size, -1)
                for term in (gain_one_grad, gain_two_grad, router_grad, table_grad)
            ],
            axis=1,
        ),
        ("fsdp", "context", "expert"),
    )
    small_share = take(small_sum, lax.axis_index("fsdp"))
    output_share = dense_reduce(output_grad)
    return (
        layer_out,
        tokens_grad,
        small_share[:gain_rows],
        inner_share[:, :model_width],
        inner_share[:, model_width : 2 * model_width],
        inner_share[:, 2 * model_width :],
        output_share,
        small_share[(2 + experts) * gain_rows :].reshape(bias_table.shape),
        small_share[gain_rows : 2 * gain_rows],
        small_share[2 * gain_rows : (2 + experts) * gain_rows].reshape(router_matrix.shape),
        expert_reduce(first_grad)[None],
        expert_reduce(second_grad)[None],
    )


def solution(mesh):
    return jax.shard_map(
        per_device,
        mesh=mesh,
        in_specs=(
            P(("fsdp", "expert"), "context", None),
            P(("fsdp", "expert"), "context", None),
            P(("fsdp", "expert"), "context"),
            P(("fsdp", "expert"), "context"),
            P(),
            P("fsdp"),
            P("fsdp", None),
            P("fsdp", None),
            P("fsdp", None),
            P("fsdp", None),
            P("fsdp", None),
            P("fsdp"),
            P("fsdp", None),
            P("expert", "fsdp", None),
            P("expert", "fsdp", None),
        ),
        out_specs=(
            P(("fsdp", "expert"), "context", None),
            P(("fsdp", "expert"), "context", None),
            P("fsdp"),
            P("fsdp", None),
            P("fsdp", None),
            P("fsdp", None),
            P("fsdp", None),
            P("fsdp", None),
            P("fsdp"),
            P("fsdp", None),
            P("expert", "fsdp", None),
            P("expert", "fsdp", None),
        ),
        check_vma=False,
    )
```

time: 2000 us -> 518 us (0.26); the launches traced: 1970 us -> 513 us
  local copies, waits for them, and re-layouts: 1170 us -> 72.2 us
  waiting for transfers between devices: 337 us -> 113 us
  matrix products: 205 us -> 84.5 us
  starting transfers between devices: 18.8 us -> 77.7 us
  blocking collectives: 137 us -> 85.9 us
  Pallas kernels: 0 us -> 47.4 us
  loops' own time: 29.9 us -> 0 us
  other arithmetic: 51.2 us -> 30.3 us
    reshape x9 -> x11, local copies, waits for them, and re-layouts: 309 us -> 3.17 us  [the longest x4 1.46 us: per_device(): term.reshape(fsdp_size, -1)]
    another operation x12 -> x2, local copies, waits for them, and re-layouts: 248 us -> 0.01 us  [gather_flat(): pair = jnp.stack((vector, near))]
    reduce_scatter x7 -> x0, waiting for transfers between devices: 203 us -> none  [the longest x1 60.4 us: per_device(): lax.psum_scatter(second_grad.astype(jnp.bfloat16), 'fsdp', scatter_dimens...]
    rev x2 -> x0, local copies, waits for them, and re-layouts: 190 us -> none  [table_terms(): flipped = grad_scores.astype(jnp.float32)[:, ::-1, :]]
    while x62 -> x0, local copies, waits for them, and re-layouts: 181 us -> none
    slice x14 -> x22, local copies, waits for them, and re-layouts: 172 us -> 7.12 us  [the longest x4 1.97 us: square_gather(): two[..., :half]]
    dot_general x31 -> x10, matrix products: 181 us -> 64.9 us  [the longest x1 10.3 us: per_device(): jnp.einsum('scd,fd->scf', grad_produced, w_second, preferred_element_type...]
    ppermute x0 -> x60, waiting for transfers between devices: none -> 73.7 us  [swap(): lax.ppermute(values, axis, [(place, place ^ distance) for place in range(...]
  transfers between devices with their start and end apart: 21 -> 64, of which waited for: 15 -> 27; matrix products, arithmetic and copies ran while one was open for 31% -> 30% of each run, Pallas kernels for 0% -> 9%
where the time goes in v1:
time: 518 us; the launch traced here: 513 us
  waiting for transfers between devices  113 us (22%)
  blocking collectives  85.9 us (17%)
  matrix products  84.5 us (16%)
  starting transfers between devices  77.7 us (15%)
  local copies, waits for them, and re-layouts  72.2 us (14%)
  Pallas kernels  47.4 us (9%)
  other arithmetic  30.3 us (6%)
    ppermute x60, waiting for transfers between devices, swap(): lax.ppermute(values, axis, [(place, place ^ distance) for place in range(...  73.7 us
    ppermute x60, starting transfers between devices, swap(): lax.ppermute(values, axis, [(place, place ^ distance) for place in range(...  59.6 us
    psum x1, blocking collectives, per_device(): lax.psum(jnp.concatenate([term.reshape(fsdp_size, -1) for term in (gain_o...  43.2 us
    psum x1, blocking collectives, sum_experts(): return lax.psum(share, 'expert')  42.7 us
    pallas_call x1, Pallas kernels, backward_call(): pl.pallas_call(functools.partial(attention_backward, width), grid=(heads...  31.8 us
    dynamic_update_slice x31, local copies, waits for them, and re-layouts, place_at(): lax.dynamic_update_slice(whole, piece[None, None], (owner, side, 0, 0))  30.9 us
    all_to_all x1, waiting for transfers between devices, per_device(): lax.all_to_all(outgoing, 'expert', split_axis=0, concat_axis=0, tiled=True)  17.6 us
    pallas_call x1, Pallas kernels, forward_call(): pl.pallas_call(functools.partial(attention_forward, width), grid=(heads /...  15.6 us
  transfers between devices with their start and end apart: 64, of which 27 were waited for; matrix products, arithmetic and copies ran while one was open for 30% of the time, Pallas kernels for 9%

profile of v1, /device:TPU:1, one launch (start us, length us, event | category | flops | bytes accessed | tf_op | source)
XLA Modules:
  0.0 513.2 jit_solution(7226808421361056777)
XLA Ops:
  51.2 7.1 %collective-permute-done.20 = bf16[96,3072]{1,0:T(8,128)(2,1)} collective-permute-done((bf16[96,3072]{1,0:T(8,128)(2,1)S(1)}, bf16[96,3072]{1,0:T(8,128)(2,1)}, u32[]{:S(2)}, u32[]{:S(2)}) %collective-permute-start.20) | collective-permute-done | bytes 589856 | tf_op jit(solution)/shard_map/ppermute | solution.py:193
  66.9 5.3 %collective-permute-done.28 = bf16[384,768]{1,0:T(8,128)(2,1)S(1)} collective-permute-done((bf16[384,768]{1,0:T(8,128)(2,1)}, bf16[384,768]{1,0:T(8,128)(2,1)S(1)}, u32[]{:S(2)}, u32[]{:S(2)}) %collective-permute-start.28) | collective-permute-done | bytes 589856 | tf_op jit(solution)/shard_map/ppermute | solution.py:193
  83.5 5.0 collective-permute-done.29
  89.5 8.5 %collective-permute-start.8 = (bf16[96,2304]{1,0:T(8,128)(2,1)}, bf16[96,2304]{1,0:T(8,128)(2,1)S(1)}, u32[]{:S(2)}, u32[]{:S(2)}) collective-permute-start(bf16[96,2304]{1,0:T(8,128)(2,1)} %collective-permute-done.3), channel_id=1, source_target_pairs={{0,4},{4,0},{1,5},{5,1},{2,6},{6,2},{3,7},{7,3},{8,12},{12,8},{9,1... | collective-permute-start | bytes 1327112 | tf_op jit(solution)/shard_map/ppermute | solution.py:193
  120.2 15.6 %attention_forward.1 = (bf16[512,768]{1,0:T(8,128)(2,1)S(1)}, f32[12,1,512]{2,1,0:T(1,128)S(1)}) custom-call(bf16[512,768]{1,0:T(8,128)(2,1)S(1)} %slice.211.query_ref, bf16[1024,768]{1,0:T(8,128)(2,1)S(1)} %get-tuple-element.49.key_ref, bf16[1024,768]{1,0:T(8,128)(2,1)S(1)} %get-tuple-element.48.value_ref, f32[12,1,1536]{2,1,0:T(1,128)S(1)} %broadcast_in_dim.181.window_ref), custom_call_target="tpu_custom_call" | custom-call | tf_op jit(solution)/shard_map/attention_forward/pallas_call | solution.py:133
  138.8 4.8 all-to-all-start
  150.1 17.6 %all-to-all-done = bf16[4,160,768]{2,1,0:T(8,128)(2,1)} async-done(((bf16[4,160,768]{2,1,0:T(8,128)(2,1)}), bf16[4,160,768]{2,1,0:T(8,128)(2,1)}, u32[]{:S(2)}, u32[]{:S(2)}) %all-to-all-start) | async-done | bytes 983072 | tf_op jit(solution)/shard_map/all_to_all | solution.py:441
  175.8 9.0 %fusion.105 = f32[4,160,3072]{2,1,0:T(8,128)} fusion(bf16[4,160,768]{2,1,0:T(8,128)(2,1)} %all-to-all-done, bf16[768,3072,1]{1,0,2:T(8,128)(2,1)} %bitcast.33), kind=kOutput, calls=%fused_computation.257 | convolution fusion | flops 3019898880 | bytes 13565952 | tf_op jit(solution)/shard_map/scd,df->scf/dot_general | solution.py:442
  184.9 10.9 %all-to-all-done.2 = bf16[4,160,768]{2,1,0:T(8,128)(2,1)} async-done(((bf16[4,160,768]{2,1,0:T(8,128)(2,1)}), bf16[4,160,768]{2,1,0:T(8,128)(2,1)}, u32[]{:S(2)}, u32[]{:S(2)}) %all-to-all-start.2) | async-done | bytes 983072 | tf_op jit(solution)/shard_map/all_to_all | solution.py:463
  195.8 10.3 %fusion.6 = bf16[4,160,3072]{2,1,0:T(8,128)(2,1)S(1)} fusion(f32[4,160,3072]{2,1,0:T(8,128)} %fusion.105, bf16[4,160,768]{2,1,0:T(8,128)(2,1)} %all-to-all-done.2, bf16[3072,768,1]{1,0,2:T(8,128)(2,1)} %bitcast.44), kind=kOutput, calls=%fused_computation.10 | convolution fusion | flops 3059220480 | bytes 17498112 | tf_op jit(solution)/shard_map/scd,fd->scf/dot_general | solution.py:464
  208.1 6.6 %convolution_convert_fusion.3 = bf16[4,160,768]{2,1,0:T(8,128)(2,1)} fusion(bf16[4,160,3072]{2,1,0:T(8,128)(2,1)S(1)} %fusion.6, bf16[768,3072,1]{1,0,2:T(8,128)(2,1)} %bitcast.33), kind=kOutput, calls=%fused_computation.57 | convolution fusion | flops 3020390400 | bytes 9633792 | tf_op jit(solution)/shard_map/scf,df->scd/dot_general | solution.py:478
  214.6 4.6 all-to-all-start.3
  219.3 6.3 %bitcast_convert_fusion.1 = bf16[768,3072]{1,0:T(8,128)(2,1)S(1)} fusion(bf16[4,160,768]{2,1,0:T(8,128)(2,1)} %all-to-all-done, bf16[4,160,3072]{2,1,0:T(8,128)(2,1)} %copy-done.51), kind=kOutput, calls=%fused_computation.3 | convolution fusion | flops 3022258176 | bytes 9633792 | tf_op jit(solution)/shard_map/scd,scf->df/dot_general | solution.py:475
  230.0 10.2 %convolution_convert_fusion.4 = bf16[4,160,768]{2,1,0:T(8,128)(2,1)} fusion(bf16[3072,768,1]{1,0,2:T(8,128)(2,1)} %bitcast.44, f32[4,160,3072]{2,1,0:T(8,128)} %fusion.105), kind=kOutput, calls=%fused_computation.58 | convolution fusion | flops 3038085120 | bytes 13565952 | tf_op jit(solution)/shard_map/scf,fd->scd/dot_general | solution.py:444
  247.6 8.4 %bitcast_convert_fusion = bf16[3072,768]{1,0:T(8,128)(2,1)S(1)} fusion(bf16[4,160,768]{2,1,0:T(8,128)(2,1)} %all-to-all-done.2, f32[4,160,3072]{2,1,0:T(8,128)} %fusion.105), kind=kOutput, calls=%fused_computation.2 | convolution fusion | flops 3039952896 | bytes 13565952 | tf_op jit(solution)/shard_map/scf,scd->fd/dot_general | solution.py:469
  263.6 7.9 %all-to-all-done.1 = bf16[4,160,768]{2,1,0:T(8,128)(2,1)} async-done(((bf16[4,160,768]{2,1,0:T(8,128)(2,1)}), bf16[4,160,768]{2,1,0:T(8,128)(2,1)}, u32[]{:S(2)}, u32[]{:S(2)}) %all-to-all-start.1) | async-done | bytes 983072 | tf_op jit(solution)/shard_map/all_to_all | solution.py:447
  279.5 31.8 %attention_backward.1 = (bf16[512,768]{1,0:T(8,128)(2,1)S(1)}, bf16[1024,768]{1,0:T(8,128)(2,1)S(1)}, bf16[1024,768]{1,0:T(8,128)(2,1)S(1)}, f32[12,1,1536]{2,1,0:T(1,128)S(1)}) custom-call(bf16[512,768]{1,0:T(8,128)(2,1)S(1)} %copy-done.1, bf16[1024,768]{1,0:T(8,128)(2,1)S(1)} %get-tuple-element.49.key_ref, ...), custom_call_target="tpu_custom_call" | custom-call | tf_op jit(solution)/shard_map/attention_backward/pallas_call | solution.py:162
  341.5 6.3 %collective-permute-done.51 = bf16[2,96,1536]{2,1,0:T(8,128)(2,1)S(1)} collective-permute-done((bf16[2,96,1536]{2,1,0:T(8,128)(2,1)S(1)}, bf16[2,96,1536]{2,1,0:T(8,128)(2,1)S(1)}, u32[]{:S(2)}, u32[]{:S(2)}) %collective-permute-start.51) | collective-permute-done | bytes 589856 | tf_op jit(solution)/shard_map/ppermute | solution.py:193
  350.6 9.8 %collective-permute-done.57 = bf16[2,384,384]{2,1,0:T(8,128)(2,1)S(1)} collective-permute-done((bf16[2,384,384]{2,1,0:T(8,128)(2,1)S(1)}, bf16[2,384,384]{2,1,0:T(8,128)(2,1)S(1)}, u32[]{:S(2)}, u32[]{:S(2)}) %collective-permute-start.57) | collective-permute-done | bytes 589856 | tf_op jit(solution)/shard_map/ppermute | solution.py:193
  365.1 5.3 %fusion.17 = (f32[768]{0:T(1024)S(1)}, f32[512]{0:T(512)S(1)}, f32[512,768]{1,0:T(8,128)}) fusion(bf16[1,512,768]{2,1,0:T(8,128)(2,1)S(1)} %copy-done.21, f32[512]{0:T(512)S(1)} %fusion.89, f32[768]{0:T(1024)S(1)} %reshape.410, bf16[768,2304]{1,0:T(8,128)(2,1)} %bitcast.10, bf16[512,1536]{1,0:T(8,128)(2,1)S(1)} %add_convert_fusion, ...), kind=kOutput, calls=%fused_computation.39 | convolution fusion | flops 1819409152 | bytes 8267776 | tf_op jit(solution)/shard_map/te,de->td/dot_general | solution.py:515
  374.5 43.2 %psum.21 = f32[4,1248]{1,0:T(4,128)S(1)} all-reduce(f32[4,1248]{1,0:T(4,128)S(1)} %concatenate.77), channel_id=1, replica_groups=mesh['fsdp'=4,'context'=2,'expert'=4] {'fsdp','context','expert'}, use_global_device_ids=true, to_apply=%region_10.11 | all-reduce | flops 4992 | bytes 39936 | tf_op jit(solution)/shard_map/psum | solution.py:520
  442.4 9.9 %collective-permute-done.39 = bf16[2,96,1152]{2,1,0:T(8,128)(2,1)S(1)} collective-permute-done((bf16[2,96,1152]{2,1,0:T(8,128)(2,1)S(1)}, bf16[2,96,1152]{2,1,0:T(8,128)(2,1)S(1)}, u32[]{:S(2)}, u32[]{:S(2)}) %collective-permute-start.39) | collective-permute-done | bytes 442400 | tf_op jit(solution)/shard_map/ppermute | solution.py:193
  460.0 42.7 %all-reduce.3 = (bf16[288,768]{1,0:T(8,128)(2,1)S(1)}, bf16[96,768]{1,0:T(8,128)(2,1)S(1)}) all-reduce(f32[288,768]{1,0:T(8,128)S(1)} %reshape.403, f32[96,768]{1,0:T(8,128)S(1)} %pad_maximum_fusion.12), channel_id=1, replica_groups=mesh['fsdp'=4,'context'=2,'expert'=4] {'expert'}, use_global_device_ids=true, to_apply=%region_11.12 | all-reduce | flops 294912 | bytes 1769472 | tf_op jit(solution)/shard_map/psum | solution.py:301
  503.1 5.9 %collective-permute-start.41 = (bf16[96,2304]{1,0:T(8,128)(2,1)S(1)}, bf16[96,2304]{1,0:T(8,128)(2,1)S(1)}, u32[]{:S(2)}, u32[]{:S(2)}) collective-permute-start(bf16[96,2304]{1,0:T(8,128)(2,1)S(1)} %convert_element_type.483), channel_id=1, source_target_pairs={{0,4},{4,0},{1,5},{5,1},{2,6},{6,2},{3,7},{7,3},{8,12},{12,8},{9,1... | collective-permute-start | bytes 1327112 | tf_op jit(solution)/shard_map/ppermute | solution.py:193
  (414 shorter events, 218.1 us)
Async XLA Ops:
  3.8 40.1 %collective-permute-start.2 = (bf16[96,2304]{1,0:T(8,128)(2,1)}, bf16[96,2304]{1,0:T(8,128)(2,1)}, u32[]{:S(2)}, u32[]{:S(2)}) collective-permute-start(bf16[96,2304]{1,0:T(8,128)(2,1)} %get-tuple-element.47), channel_id=1, source_target_pairs={{0,8},{8,0},{16,24},{24,16},{1,9},{9,1},{17,25},{25,17},{2,10},{10... | collective-permute-start | bytes 1327112 | tf_op jit(solution)/shard_map/ppermute | solution.py:193
  5.9 41.6 %collective-permute-start.3 = (bf16[96,2304]{1,0:T(8,128)(2,1)}, bf16[96,2304]{1,0:T(8,128)(2,1)}, u32[]{:S(2)}, u32[]{:S(2)}) collective-permute-start(bf16[96,2304]{1,0:T(8,128)(2,1)} %get-tuple-element.47), channel_id=1, source_target_pairs={{0,16},{8,24},{16,0},{24,8},{1,17},{9,25},{17,1},{25,9},{2,18},{10... | collective-permute-start | bytes 1327112 | tf_op jit(solution)/shard_map/ppermute | solution.py:193
  7.1 71.8 %collective-permute-start.6 = (bf16[96,2304]{1,0:T(8,128)(2,1)}, bf16[96,2304]{1,0:T(8,128)(2,1)}, u32[]{:S(2)}, u32[]{:S(2)}) collective-permute-start(bf16[96,2304]{1,0:T(8,128)(2,1)} %get-tuple-element.47), channel_id=1, source_target_pairs={{0,4},{4,0},{1,5},{5,1},{2,6},{6,2},{3,7},{7,3},{8,12},{12,8},{9,1... | collective-permute-start | bytes 1327112 | tf_op jit(solution)/shard_map/ppermute | solution.py:193
  37.0 22.6 %collective-permute-start.19 = (bf16[96,3072]{1,0:T(8,128)(2,1)}, bf16[96,3072]{1,0:T(8,128)(2,1)S(1)}, u32[]{:S(2)}, u32[]{:S(2)}) collective-permute-start(bf16[96,3072]{1,0:T(8,128)(2,1)} %dynamic-slice_bitcast_fusion.5), channel_id=1, source_target_pairs={{0,8},{8,0},{16,24},{24,16},{1,9},{9,1},{17,25},{25,17},{2,10},{10... | collective-permute-start | bytes 1769480 | tf_op jit(solution)/shard_map/ppermute | solution.py:193
  44.0 62.0 %collective-permute-start.23 = (bf16[96,3072]{1,0:T(8,128)(2,1)S(1)}, bf16[96,3072]{1,0:T(8,128)(2,1)S(1)}, u32[]{:S(2)}, u32[]{:S(2)}) collective-permute-start(bf16[96,3072]{1,0:T(8,128)(2,1)S(1)} %copy-done.32), channel_id=1, source_target_pairs={{0,4},{4,0},{1,5},{5,1},{2,6},{6,2},{3,7},{7,3},{8,12},{12,8},{9,1... | collective-permute-start | bytes 1769480 | tf_op jit(solution)/shard_map/ppermute | solution.py:193
  59.6 55.7 %collective-permute-start.31 = (bf16[384,768]{1,0:T(8,128)(2,1)}, bf16[384,768]{1,0:T(8,128)(2,1)S(1)}, u32[]{:S(2)}, u32[]{:S(2)}) collective-permute-start(bf16[384,768]{1,0:T(8,128)(2,1)} %dynamic-slice_bitcast_fusion.4), channel_id=1, source_target_pairs={{0,4},{4,0},{1,5},{5,1},{2,6},{6,2},{3,7},{7,3},{8,12},{12,8},{9,1... | collective-permute-start | bytes 1769480 | tf_op jit(solution)/shard_map/ppermute | solution.py:193
  73.3 30.5 %collective-permute-start.7 = (bf16[96,2304]{1,0:T(8,128)(2,1)}, bf16[96,2304]{1,0:T(8,128)(2,1)S(1)}, u32[]{:S(2)}, u32[]{:S(2)}) collective-permute-start(bf16[96,2304]{1,0:T(8,128)(2,1)} %collective-permute-done.2), channel_id=1, source_target_pairs={{0,4},{4,0},{1,5},{5,1},{2,6},{6,2},{3,7},{7,3},{8,12},{12,8},{9,1... | collective-permute-start | bytes 1327112 | tf_op jit(solution)/shard_map/ppermute | solution.py:193
  98.7 20.2 %collective-permute-start.24 = (bf16[96,3072]{1,0:T(8,128)(2,1)S(1)}, bf16[96,3072]{1,0:T(8,128)(2,1)S(1)}, u32[]{:S(2)}, u32[]{:S(2)}) collective-permute-start(bf16[96,3072]{1,0:T(8,128)(2,1)S(1)} %collective-permute-done.19), channel_id=1, source_target_pairs={{0,4},{4,0},{1,5},{5,1},{2,6},{6,2},{3,7},{7,3},{8,12},{12,8},{9,1... | collective-permute-start | bytes 1769480 | tf_op jit(solution)/shard_map/ppermute | solution.py:193
  115.2 28.3 %collective-permute-start.25 = (bf16[96,3072]{1,0:T(8,128)(2,1)}, bf16[96,3072]{1,0:T(8,128)(2,1)}, u32[]{:S(2)}, u32[]{:S(2)}) collective-permute-start(bf16[96,3072]{1,0:T(8,128)(2,1)} %collective-permute-done.20), channel_id=1, source_target_pairs={{0,4},{4,0},{1,5},{5,1},{2,6},{6,2},{3,7},{7,3},{8,12},{12,8},{9,1... | collective-permute-start | bytes 1769480 | tf_op jit(solution)/shard_map/ppermute | solution.py:193
  116.6 57.2 %collective-permute-start.26 = (bf16[96,3072]{1,0:T(8,128)(2,1)}, bf16[96,3072]{1,0:T(8,128)(2,1)}, u32[]{:S(2)}, u32[]{:S(2)}) collective-permute-start(bf16[96,3072]{1,0:T(8,128)(2,1)} %constant_dynamic-update-slice_fusion.7), channel_id=1, source_target_pairs={{0,4},{4,0},{1,5},{5,1},{2,6},{6,2},{3,7},{7,3},{8,12},{12,8},{9,1... | collective-permute-start | bytes 1769480 | tf_op jit(solution)/shard_map/ppermute | solution.py:193
  117.7 54.2 %collective-permute-start.34 = (bf16[384,768]{1,0:T(8,128)(2,1)}, bf16[384,768]{1,0:T(8,128)(2,1)}, u32[]{:S(2)}, u32[]{:S(2)}) collective-permute-start(bf16[384,768]{1,0:T(8,128)(2,1)} %constant_dynamic-update-slice_fusion.9), channel_id=1, source_target_pairs={{0,4},{4,0},{1,5},{5,1},{2,6},{6,2},{3,7},{7,3},{8,12},{12,8},{9,1... | collective-permute-start | bytes 1769480 | tf_op jit(solution)/shard_map/ppermute | solution.py:193
  138.8 28.9 %all-to-all-start = ((bf16[4,160,768]{2,1,0:T(8,128)(2,1)}), bf16[4,160,768]{2,1,0:T(8,128)(2,1)}, u32[]{:S(2)}, u32[]{:S(2)}) async-start(bf16[4,160,768]{2,1,0:T(8,128)(2,1)} %bitcast.274), calls=%async_computation | async-start | bytes 1966080 | tf_op jit(solution)/shard_map/all_to_all | solution.py:441
  167.6 28.1 %all-to-all-start.2 = ((bf16[4,160,768]{2,1,0:T(8,128)(2,1)}), bf16[4,160,768]{2,1,0:T(8,128)(2,1)}, u32[]{:S(2)}, u32[]{:S(2)}) async-start(bf16[4,160,768]{2,1,0:T(8,128)(2,1)} %bitcast.273), calls=%async_computation.2 | async-start | bytes 1966080 | tf_op jit(solution)/shard_map/all_to_all | solution.py:463
  214.6 28.5 %all-to-all-start.3 = ((bf16[4,160,768]{2,1,0:T(8,128)(2,1)}), bf16[4,160,768]{2,1,0:T(8,128)(2,1)}, u32[]{:S(2)}, u32[]{:S(2)}) async-start(bf16[4,160,768]{2,1,0:T(8,128)(2,1)} %convolution_convert_fusion.3), calls=%async_computation.3 | async-start | bytes 1966080 | tf_op jit(solution)/shard_map/all_to_all | solution.py:481
  228.6 102.9 %collective-permute-start.48 = (bf16[4,96,3072]{2,1,0:T(8,128)(2,1)}, bf16[4,96,3072]{2,1,0:T(8,128)(2,1)}, u32[]{:S(2)}, u32[]{:S(2)}) collective-permute-start(bf16[4,96,3072]{2,1,0:T(8,128)(2,1)} %dynamic-slice_bitcast_fusion.1), channel_id=1, source_target_pairs={{0,4},{4,0},{1,5},{5,1},{2,6},{6,2},{3,7},{7,3},{8,12},{12,8},{9,1... | collective-permute-start | bytes 7077896 | tf_op jit(solution)/shard_map/ppermute | solution.py:193
  243.2 28.3 %all-to-all-start.1 = ((bf16[4,160,768]{2,1,0:T(8,128)(2,1)}), bf16[4,160,768]{2,1,0:T(8,128)(2,1)}, u32[]{:S(2)}, u32[]{:S(2)}) async-start(bf16[4,160,768]{2,1,0:T(8,128)(2,1)} %convolution_convert_fusion.4), calls=%async_computation.1 | async-start | bytes 1966080 | tf_op jit(solution)/shard_map/all_to_all | solution.py:447
  258.9 77.9 %collective-permute-start.54 = (bf16[4,384,768]{2,1,0:T(8,128)(2,1)}, bf16[4,384,768]{2,1,0:T(8,128)(2,1)}, u32[]{:S(2)}, u32[]{:S(2)}) collective-permute-start(bf16[4,384,768]{2,1,0:T(8,128)(2,1)} %dynamic-slice_bitcast_fusion), channel_id=1, source_target_pairs={{0,4},{4,0},{1,5},{5,1},{2,6},{6,2},{3,7},{7,3},{8,12},{12,8},{9,1... | collective-permute-start | bytes 7077896 | tf_op jit(solution)/shard_map/ppermute | solution.py:193
  315.2 48.1 %collective-permute-start.35 = (bf16[512,1536]{1,0:T(8,128)(2,1)}, bf16[512,1536]{1,0:T(8,128)(2,1)}, u32[]{:S(2)}, u32[]{:S(2)}) collective-permute-start(bf16[512,1536]{1,0:T(8,128)(2,1)} %constant_dynamic-slice_fusion.17), channel_id=1, source_target_pairs={{0,4},{4,0},{1,5},{5,1},{2,6},{6,2},{3,7},{7,3},{8,12},{12,8},{9,1... | collective-permute-start | bytes 4718600 | tf_op jit(solution)/shard_map/ppermute | solution.py:193
  339.4 20.9 %collective-permute-start.57 = (bf16[2,384,384]{2,1,0:T(8,128)(2,1)S(1)}, bf16[2,384,384]{2,1,0:T(8,128)(2,1)S(1)}, u32[]{:S(2)}, u32[]{:S(2)}) collective-permute-start(bf16[2,384,384]{2,1,0:T(8,128)(2,1)S(1)} %pad_maximum_fusion.8), channel_id=1, source_target_pairs={{0,16},{8,24},{16,0},{24,8},{1,17},{9,25},{17,1},{25,9},{2,18},{10... | collective-permute-start | bytes 1769480 | tf_op jit(solution)/shard_map/ppermute | solution.py:193
  340.1 21.2 %collective-permute-start.55 = (bf16[2,384,384]{2,1,0:T(8,128)(2,1)S(1)}, bf16[2,384,384]{2,1,0:T(8,128)(2,1)S(1)}, u32[]{:S(2)}, u32[]{:S(2)}) collective-permute-start(bf16[2,384,384]{2,1,0:T(8,128)(2,1)S(1)} %pad_maximum_fusion.7), channel_id=1, source_target_pairs={{0,8},{8,0},{16,24},{24,16},{1,9},{9,1},{17,25},{25,17},{2,10},{10... | collective-permute-start | bytes 1769480 | tf_op jit(solution)/shard_map/ppermute | solution.py:193
  348.6 81.2 %collective-permute-start.52 = (bf16[96,1536]{1,0:T(8,128)(2,1)}, bf16[96,1536]{1,0:T(8,128)(2,1)}, u32[]{:S(2)}, u32[]{:S(2)}) collective-permute-start(bf16[96,1536]{1,0:T(8,128)(2,1)} %fusion.71), channel_id=1, source_target_pairs={{0,8},{8,0},{16,24},{24,16},{1,9},{9,1},{17,25},{25,17},{2,10},{10... | collective-permute-start | bytes 884744 | tf_op jit(solution)/shard_map/ppermute | solution.py:193
  349.5 81.5 %collective-permute-start.50 = (bf16[96,1536]{1,0:T(8,128)(2,1)}, bf16[96,1536]{1,0:T(8,128)(2,1)}, u32[]{:S(2)}, u32[]{:S(2)}) collective-permute-start(bf16[96,1536]{1,0:T(8,128)(2,1)} %fusion.70), channel_id=1, source_target_pairs={{0,16},{8,24},{16,0},{24,8},{1,17},{9,25},{17,1},{25,9},{2,18},{10... | collective-permute-start | bytes 884744 | tf_op jit(solution)/shard_map/ppermute | solution.py:193
  361.2 65.9 %collective-permute-start.58 = (bf16[384,384]{1,0:T(8,128)(2,1)}, bf16[384,384]{1,0:T(8,128)(2,1)}, u32[]{:S(2)}, u32[]{:S(2)}) collective-permute-start(bf16[384,384]{1,0:T(8,128)(2,1)} %fusion.73), channel_id=1, source_target_pairs={{0,8},{8,0},{16,24},{24,16},{1,9},{9,1},{17,25},{25,17},{2,10},{10... | collective-permute-start | bytes 884744 | tf_op jit(solution)/shard_map/ppermute | solution.py:193
  362.1 66.3 %collective-permute-start.56 = (bf16[384,384]{1,0:T(8,128)(2,1)}, bf16[384,384]{1,0:T(8,128)(2,1)}, u32[]{:S(2)}, u32[]{:S(2)}) collective-permute-start(bf16[384,384]{1,0:T(8,128)(2,1)} %fusion.72), channel_id=1, source_target_pairs={{0,16},{8,24},{16,0},{24,8},{1,17},{9,25},{17,1},{25,9},{2,18},{10... | collective-permute-start | bytes 884744 | tf_op jit(solution)/shard_map/ppermute | solution.py:193
  (94 other events, 833.5 us)

commit v2 on v1

--- a/solution.py
+++ b/solution.py
@@ -227,16 +227,49 @@
     half = rows // 2
     mine = square_gather(lax.dynamic_slice_in_dim(shard, core * half, half, 0))
     theirs = [swap(piece, "context", 1) for piece in mine]
-    whole = jnp.zeros((4, 2, half, columns), shard.dtype)
-
-    def place_at(side):
-        return lambda whole, piece, owner: lax.dynamic_update_slice(
-            whole, piece[None, None], (owner, side, 0, 0)
+    return assemble(mine, theirs).reshape(4 * rows, columns)
+
+
+def assemble_copies(*refs):
+    piece_refs, whole_ref, arrived = refs[:8], refs[8], refs[9]
+    row = lax.axis_index("fsdp")
+    core = lax.axis_index("context")
+    copies = [
+        pltpu.make_async_copy(
+            piece_refs[4 * side + distance],
+            whole_ref.at[row ^ distance, (1 - core) if side else core],
+            arrived.at[4 * side + distance],
         )
-
-    whole = place_pieces(mine, whole, place_at(core))
-    whole = place_pieces(theirs, whole, place_at(1 - core))
-    return whole.reshape(4 * rows, columns)
+        for side in range(2)
+        for distance in range(4)
+    ]
+    for copy in copies:
+        copy.start()
+    for copy in copies:
+        copy.wait()
+
+
+def assemble(mine, theirs):
+    half, columns = mine[0].shape
+    return pl.pallas_call(
+        assemble_copies,
+        in_specs=[pl.BlockSpec(memory_space=pl.ANY)] * 8,
+        out_specs=pl.BlockSpec(memory_space=pl.ANY),
+        out_shape=jax.ShapeDtypeStruct((4, 2, half, columns), mine[0].dtype),
+        scratch_shapes=[pltpu.SemaphoreType.DMA((8,))],
+        name="assemble",
+    )(*mine, *theirs)
+
+
+def small_reduce(terms):
+    row = lax.axis_index("fsdp")
+    if lax.axis_size("fsdp") != 4 or not paired() or lax.axis_size("expert") != 4:
+        return take(lax.psum(terms, ("fsdp", "context", "expert")), row)
+    came = swap(jnp.stack((take(terms, row ^ 1), take(terms, row ^ 3))), "fsdp", 1)
+    own = take(terms, row) + came[0] + swap(take(terms, row ^ 2) + came[1], "fsdp", 2)
+    own = own + swap(own, "context", 1)
+    own = own + swap(own, "expert", 1)
+    return own + swap(own, "expert", 2)
 
 
 def gather_flat(vector):
@@ -297,7 +330,7 @@
 def sum_experts(share):
     size = lax.axis_size("expert")
     rows, columns = share.shape
-    if size != 4 or rows % 64:
+    if size != 4 or rows % 4:
         return lax.psum(share, "expert")
     row = lax.axis_index("expert")
     blocks = share.astype(low).reshape(4, rows // 4, columns)
@@ -394,9 +427,12 @@
     w_router = small[:, 2 * gain_rows : (2 + experts) * gain_rows].reshape(-1, experts)
     table_rows = small[:, (2 + experts) * gain_rows :].reshape(-1, bias_table.shape[1])
     w_inner = gather_rows(jnp.concatenate((query_weight, key_weight, value_weight), axis=1))
-    w_output = gather_rows(attention_output_matrix)
-    w_first = gather_rows(expert_in[0])
-    w_second = gather_rows(expert_out[0])
+    w_inner, output_shard, first_shard, second_shard = lax.optimization_barrier(
+        (w_inner, attention_output_matrix, expert_in[0], expert_out[0])
+    )
+    w_output = gather_rows(output_shard)
+    w_first = gather_rows(first_shard)
+    w_second = gather_rows(second_shard)
     head_count = table_rows.shape[1]
     head_dim = model_width // head_count
     bucket_count = table_rows.shape[0]
@@ -517,17 +553,15 @@
     tokens_grad = (grad_middle + grad_inputs_norm).astype(jnp.bfloat16).reshape(tokens.shape)
     layer_out = layer_sum.astype(jnp.bfloat16).reshape(tokens.shape)
     fsdp_size = lax.axis_size("fsdp")
-    small_sum = lax.psum(
+    small_share = small_reduce(
         jnp.concatenate(
             [
                 term.reshape(fsdp_size, -1)
                 for term in (gain_one_grad, gain_two_grad, router_grad, table_grad)
             ],
             axis=1,
-        ),
-        ("fsdp", "context", "expert"),
-    )
-    small_share = take(small_sum, lax.axis_index("fsdp"))
+        )
+    )
     output_share = dense_reduce(output_grad)
     return (
         layer_out,

time: 518 us -> 854 us (1.65)
  Pallas kernels: 47.4 us -> 481 us
  blocking collectives: 85.9 us -> 0 us
  starting transfers between devices: 77.7 us -> 102 us
  local copies, waits for them, and re-layouts: 72.2 us -> 52.8 us
  waiting for transfers between devices: 113 us -> 95.9 us
    pallas_call x0 -> x4, Pallas kernels: none -> 434 us  [assemble(): pl.pallas_call(assemble_copies, in_specs=[pl.BlockSpec(memory_space=pl.AN...]
    psum x2 -> x0, blocking collectives: 85.9 us -> none  [the longest x1 43.2 us: per_device(): lax.psum(jnp.concatenate([term.reshape(fsdp_size, -1) for term in (gain_o...]
    dynamic_update_slice x31 -> x6, local copies, waits for them, and re-layouts: 30.9 us -> 0.05 us  [sum_experts(): whole = lax.dynamic_update_slice(whole, came[None], (row ^ distance, 0, 0))]
    ppermute x60 -> x77, starting transfers between devices: 59.6 us -> 83.3 us  [swap(): lax.ppermute(values, axis, [(place, place ^ distance) for place in range(...]
    all_to_all x1, waiting for transfers between devices: 10.9 us -> 0.01 us  [per_device(): lax.all_to_all(grad_slots, 'expert', split_axis=0, concat_axis=0, tiled=T...]
    all_to_all x1, waiting for transfers between devices: 17.6 us -> 8.45 us  [per_device(): lax.all_to_all(outgoing, 'expert', split_axis=0, concat_axis=0, tiled=True)]
    ppermute x60 -> x77, waiting for transfers between devices: 73.7 us -> 76.6 us  [swap(): lax.ppermute(values, axis, [(place, place ^ distance) for place in range(...]
  transfers between devices with their start and end apart: 64 -> 81, of which waited for: 27 -> 26; matrix products, arithmetic and copies ran while one was open for 30% -> 15% of each run, Pallas kernels for 9% -> 44%
where the time goes in v2:
time: 854 us; the launch traced here: 845 us
  Pallas kernels  481 us (56%)
  starting transfers between devices  102 us (12%)
  waiting for transfers between devices  95.9 us (11%)
  matrix products  78.5 us (9%)
  local copies, waits for them, and re-layouts  52.8 us (6%)
  other arithmetic  32.2 us (4%)
    pallas_call x4, Pallas kernels, assemble(): pl.pallas_call(assemble_copies, in_specs=[pl.BlockSpec(memory_space=pl.AN...  434 us
    ppermute x77, starting transfers between devices, swap(): lax.ppermute(values, axis, [(place, place ^ distance) for place in range(...  83.3 us
    ppermute x77, waiting for transfers between devices, swap(): lax.ppermute(values, axis, [(place, place ^ distance) for place in range(...  76.6 us
    pallas_call x1, Pallas kernels, backward_call(): pl.pallas_call(functools.partial(attention_backward, width), grid=(heads...  31.8 us
  transfers between devices with their start and end apart: 81, of which 26 were waited for; matrix products, arithmetic and copies ran while one was open for 15% of the time, Pallas kernels for 44%

profile of v2, /device:TPU:1, one launch (start us, length us, event | category | flops | bytes accessed | tf_op | source)
XLA Modules:
  0.0 844.9 jit_solution(14526956595495917502)
XLA Ops:
  10.3 4.6 collective-permute-done
  28.7 108.4 %assemble.4 = bf16[4,2,96,2304]{3,2,1,0:T(8,128)(2,1)} custom-call(bf16[96,2304]{1,0:T(8,128)(2,1)} %copy-done.29, bf16[96,2304]{1,0:T(8,128)(2,1)} %copy-done.38, bf16[96,2304]{1,0:T(8,128)(2,1)} %copy-done.37, bf16[96,2304]{1,0:T(8,128)(2,1)} %constant_dynamic-update-slice_fusion.refs_3_, bf16[96,2304]{1,0:T(8,128)(2,1)} %collective-permute-done.6.refs_4_, ...), custom_call_target="tpu_custom_call" | custom-call | tf_op jit(solution)/shard_map/assemble/pallas_call | solution.py:254
  157.7 8.1 collective-permute-done.14
  174.1 36.9 %assemble.5 = bf16[4,2,96,768]{3,2,1,0:T(8,128)(2,1)} custom-call(bf16[96,768]{1,0:T(8,128)(2,1)} %copy-done.41, bf16[96,768]{1,0:T(8,128)(2,1)} %copy-done.47, bf16[96,768]{1,0:T(8,128)(2,1)} %copy-done.48, bf16[96,768]{1,0:T(8,128)(2,1)} %copy-done.49, bf16[96,768]{1,0:T(8,128)(2,1)} %copy-done.51, bf16[96,768]{1,0:T(8,128)(2,1)} %copy-done.52, ...), custom_call_target="tpu_custom_call" | custom-call | tf_op jit(solution)/shard_map/assemble/pallas_call | solution.py:254
  217.9 15.6 %attention_forward.1 = (bf16[512,768]{1,0:T(8,128)(2,1)S(1)}, f32[12,1,512]{2,1,0:T(1,128)S(1)}) custom-call(bf16[512,768]{1,0:T(8,128)(2,1)S(1)} %copy-done.2, bf16[1024,768]{1,0:T(8,128)(2,1)S(1)} %get-tuple-element.57.key_ref, bf16[1024,768]{1,0:T(8,128)(2,1)S(1)} %get-tuple-element.56.value_ref, f32[12,1,1536]{2,1,0:T(1,128)S(1)} %broadcast_in_dim.90.window_ref), custom_call_target="tpu_custom_call" | custom-call | tf_op jit(solution)/shard_map/attention_forward/pallas_call | solution.py:133
  237.6 4.8 all-to-all-start
  257.9 8.4 %all-to-all-done = bf16[4,160,768]{2,1,0:T(8,128)(2,1)} async-done(((bf16[4,160,768]{2,1,0:T(8,128)(2,1)}), bf16[4,160,768]{2,1,0:T(8,128)(2,1)}, u32[]{:S(2)}, u32[]{:S(2)}) %all-to-all-start) | async-done | bytes 983072 | tf_op jit(solution)/shard_map/all_to_all | solution.py:477
  276.0 144.1 %assemble.6 = bf16[4,2,96,3072]{3,2,1,0:T(8,128)(2,1)} custom-call(bf16[96,3072]{1,0:T(8,128)(2,1)} %constant_dynamic-slice_fusion.22.refs_0_, bf16[96,3072]{1,0:T(8,128)(2,1)} %collective-permute-done.19.refs_1_, bf16[96,3072]{1,0:T(8,128)(2,1)} %copy-done.33, bf16[96,3072]{1,0:T(8,128)(2,1)} %copy-done.34, ...), custom_call_target="tpu_custom_call" | custom-call | tf_op jit(solution)/shard_map/assemble/pallas_call | solution.py:254
  420.2 144.1 %assemble.7 = bf16[4,2,384,768]{3,2,1,0:T(8,128)(2,1)} custom-call(bf16[384,768]{1,0:T(8,128)(2,1)} %constant_dynamic-slice_fusion.21.refs_0_, bf16[384,768]{1,0:T(8,128)(2,1)} %collective-permute-done.27.refs_1_, bf16[384,768]{1,0:T(8,128)(2,1)} %collective-permute-done.28.refs_2_, bf16[384,768]{1,0:T(8,128)(2,1)} %constant_dynamic-update-slice_fusion.6.refs_3_, ...), custom_call_target="tpu_custom_call" | custom-call | tf_op jit(solution)/shard_map/assemble/pallas_call | solution.py:254
  564.3 9.0 %fusion.116 = f32[4,160,3072]{2,1,0:T(8,128)} fusion(bf16[4,160,768]{2,1,0:T(8,128)(2,1)} %all-to-all-done, bf16[768,3072,1]{1,0,2:T(8,128)(2,1)} %bitcast.222), kind=kOutput, calls=%fused_computation.260 | convolution fusion | flops 3019898880 | bytes 13565952 | tf_op jit(solution)/shard_map/scd,df->scf/dot_general | solution.py:478
  573.4 10.4 %fusion.6 = bf16[4,160,3072]{2,1,0:T(8,128)(2,1)S(1)} fusion(f32[4,160,3072]{2,1,0:T(8,128)} %fusion.116, bf16[4,160,768]{2,1,0:T(8,128)(2,1)} %all-to-all-done.2, bf16[3072,768,1]{1,0,2:T(8,128)(2,1)} %bitcast.224), kind=kOutput, calls=%fused_computation.10 | convolution fusion | flops 3059220480 | bytes 17498112 | tf_op jit(solution)/shard_map/scd,fd->scf/dot_general | solution.py:500
  585.7 6.6 convolution_convert_fusion.3
  592.3 5.2 all-to-all-start.3
  597.5 6.3 bitcast_convert_fusion.1
  608.3 10.2 %convolution_convert_fusion.4 = bf16[4,160,768]{2,1,0:T(8,128)(2,1)} fusion(bf16[3072,768,1]{1,0,2:T(8,128)(2,1)} %bitcast.225, f32[4,160,3072]{2,1,0:T(8,128)} %fusion.116), kind=kOutput, calls=%fused_computation.54 | convolution fusion | flops 3038085120 | bytes 13565952 | tf_op jit(solution)/shard_map/scf,fd->scd/dot_general | solution.py:480
  621.5 4.4 all-to-all-start.1
  625.9 8.4 bitcast_convert_fusion
  641.9 7.9 all-to-all-done.1
  658.2 31.8 %attention_backward.1 = (bf16[512,768]{1,0:T(8,128)(2,1)S(1)}, bf16[1024,768]{1,0:T(8,128)(2,1)S(1)}, bf16[1024,768]{1,0:T(8,128)(2,1)S(1)}, f32[12,1,1536]{2,1,0:T(1,128)S(1)}) custom-call(bf16[512,768]{1,0:T(8,128)(2,1)S(1)} %copy-done.3, bf16[1024,768]{1,0:T(8,128)(2,1)S(1)} %get-tuple-element.57.key_ref, ...), custom_call_target="tpu_custom_call" | custom-call | tf_op jit(solution)/shard_map/attention_backward/pallas_call | solution.py:162
  733.4 7.1 collective-permute-done.68
  743.4 9.7 %collective-permute-done.74 = bf16[2,384,384]{2,1,0:T(8,128)(2,1)S(1)} collective-permute-done((bf16[2,384,384]{2,1,0:T(8,128)(2,1)S(1)}, bf16[2,384,384]{2,1,0:T(8,128)(2,1)S(1)}, u32[]{:S(2)}, u32[]{:S(2)}) %collective-permute-start.74) | collective-permute-done | bytes 589856 | tf_op jit(solution)/shard_map/ppermute | solution.py:193
  797.7 10.3 %collective-permute-done.44 = bf16[2,96,1152]{2,1,0:T(8,128)(2,1)S(1)} collective-permute-done((bf16[2,96,1152]{2,1,0:T(8,128)(2,1)S(1)}, bf16[2,96,1152]{2,1,0:T(8,128)(2,1)S(1)}, u32[]{:S(2)}, u32[]{:S(2)}) %collective-permute-start.44) | collective-permute-done | bytes 442400 | tf_op jit(solution)/shard_map/ppermute | solution.py:193
  809.6 4.7 collective-permute-done.45
  820.7 6.2 collective-permute-done.47
  (458 shorter events, 229.0 us)
Async XLA Ops:
  144.6 68.4 %collective-permute-start.10 = (bf16[512,1536]{1,0:T(8,128)(2,1)S(1)}, bf16[512,1536]{1,0:T(8,128)(2,1)}, u32[]{:S(2)}, u32[]{:S(2)}) collective-permute-start(bf16[512,1536]{1,0:T(8,128)(2,1)S(1)} %get-tuple-element.62), channel_id=1, source_target_pairs={{0,4},{4,0},{1,5},{5,1},{2,6},{6,2},{3,7},{7,3},{8,12},{12,8},{9,1... | collective-permute-start | bytes 4718600 | tf_op jit(solution)/shard_map/ppermute | solution.py:193
  148.6 62.5 %collective-permute-start.20 = (bf16[96,3072]{1,0:T(8,128)(2,1)}, bf16[96,3072]{1,0:T(8,128)(2,1)S(1)}, u32[]{:S(2)}, u32[]{:S(2)}) collective-permute-start(bf16[96,3072]{1,0:T(8,128)(2,1)} %constant_dynamic-slice_fusion.22.refs_0_), channel_id=1, source_target_pairs={{0,16},{8,24},{16,0},{24,8},{1,17},{9,25},{17,1},{25,9},{2,18},{10... | collective-permute-start | bytes 1769480 | tf_op jit(solution)/shard_map/ppermute | solution.py:193
  171.1 71.3 %collective-permute-start.19 = (bf16[96,3072]{1,0:T(8,128)(2,1)}, bf16[96,3072]{1,0:T(8,128)(2,1)}, u32[]{:S(2)}, u32[]{:S(2)}) collective-permute-start(bf16[96,3072]{1,0:T(8,128)(2,1)} %constant_dynamic-slice_fusion.22.refs_0_), channel_id=1, source_target_pairs={{0,8},{8,0},{16,24},{24,16},{1,9},{9,1},{17,25},{25,17},{2,10},{10... | collective-permute-start | bytes 1769480 | tf_op jit(solution)/shard_map/ppermute | solution.py:193
  172.5 75.9 %collective-permute-start.27 = (bf16[384,768]{1,0:T(8,128)(2,1)}, bf16[384,768]{1,0:T(8,128)(2,1)}, u32[]{:S(2)}, u32[]{:S(2)}) collective-permute-start(bf16[384,768]{1,0:T(8,128)(2,1)} %constant_dynamic-slice_fusion.21.refs_0_), channel_id=1, source_target_pairs={{0,8},{8,0},{16,24},{24,16},{1,9},{9,1},{17,25},{25,17},{2,10},{10... | collective-permute-start | bytes 1769480 | tf_op jit(solution)/shard_map/ppermute | solution.py:193
  172.7 74.5 %collective-permute-start.28 = (bf16[384,768]{1,0:T(8,128)(2,1)}, bf16[384,768]{1,0:T(8,128)(2,1)}, u32[]{:S(2)}, u32[]{:S(2)}) collective-permute-start(bf16[384,768]{1,0:T(8,128)(2,1)} %constant_dynamic-slice_fusion.21.refs_0_), channel_id=1, source_target_pairs={{0,16},{8,24},{16,0},{24,8},{1,17},{9,25},{17,1},{25,9},{2,18},{10... | collective-permute-start | bytes 1769480 | tf_op jit(solution)/shard_map/ppermute | solution.py:193
  211.8 39.5 %collective-permute-start.21 = (bf16[96,1536]{1,0:T(8,128)(2,1)}, bf16[96,1536]{1,0:T(8,128)(2,1)}, u32[]{:S(2)}, u32[]{:S(2)}) collective-permute-start(bf16[96,1536]{1,0:T(8,128)(2,1)} %slice.240), channel_id=1, source_target_pairs={{0,8},{8,0},{16,24},{24,16},{1,9},{9,1},{17,25},{25,17},{2,10},{10... | collective-permute-start | bytes 884744 | tf_op jit(solution)/shard_map/ppermute | solution.py:193
  237.6 28.7 %all-to-all-start = ((bf16[4,160,768]{2,1,0:T(8,128)(2,1)}), bf16[4,160,768]{2,1,0:T(8,128)(2,1)}, u32[]{:S(2)}, u32[]{:S(2)}) async-start(bf16[4,160,768]{2,1,0:T(8,128)(2,1)} %bitcast.237), calls=%async_computation | async-start | bytes 1966080 | tf_op jit(solution)/shard_map/all_to_all | solution.py:477
  245.2 30.2 %collective-permute-start.23 = (bf16[96,3072]{1,0:T(8,128)(2,1)}, bf16[96,3072]{1,0:T(8,128)(2,1)}, u32[]{:S(2)}, u32[]{:S(2)}) collective-permute-start(bf16[96,3072]{1,0:T(8,128)(2,1)} %constant_dynamic-slice_fusion.22.refs_0_), channel_id=1, source_target_pairs={{0,4},{4,0},{1,5},{5,1},{2,6},{6,2},{3,7},{7,3},{8,12},{12,8},{9,1... | collective-permute-start | bytes 1769480 | tf_op jit(solution)/shard_map/ppermute | solution.py:193
  257.9 162.3 %collective-permute-start.31 = (bf16[384,768]{1,0:T(8,128)(2,1)}, bf16[384,768]{1,0:T(8,128)(2,1)}, u32[]{:S(2)}, u32[]{:S(2)}) collective-permute-start(bf16[384,768]{1,0:T(8,128)(2,1)} %constant_dynamic-slice_fusion.21.refs_0_), channel_id=1, source_target_pairs={{0,4},{4,0},{1,5},{5,1},{2,6},{6,2},{3,7},{7,3},{8,12},{12,8},{9,1... | collective-permute-start | bytes 1769480 | tf_op jit(solution)/shard_map/ppermute | solution.py:193
  266.3 307.0 %all-to-all-start.2 = ((bf16[4,160,768]{2,1,0:T(8,128)(2,1)}), bf16[4,160,768]{2,1,0:T(8,128)(2,1)}, u32[]{:S(2)}, u32[]{:S(2)}) async-start(bf16[4,160,768]{2,1,0:T(8,128)(2,1)} %bitcast.236), calls=%async_computation.2 | async-start | bytes 1966080 | tf_op jit(solution)/shard_map/all_to_all | solution.py:499
  275.4 144.7 %collective-permute-start.32 = (bf16[384,768]{1,0:T(8,128)(2,1)}, bf16[384,768]{1,0:T(8,128)(2,1)}, u32[]{:S(2)}, u32[]{:S(2)}) collective-permute-start(bf16[384,768]{1,0:T(8,128)(2,1)} %collective-permute-done.27.refs_1_), channel_id=1, source_target_pairs={{0,4},{4,0},{1,5},{5,1},{2,6},{6,2},{3,7},{7,3},{8,12},{12,8},{9,1... | collective-permute-start | bytes 1769480 | tf_op jit(solution)/shard_map/ppermute | solution.py:193
  275.4 144.7 %collective-permute-start.33 = (bf16[384,768]{1,0:T(8,128)(2,1)}, bf16[384,768]{1,0:T(8,128)(2,1)}, u32[]{:S(2)}, u32[]{:S(2)}) collective-permute-start(bf16[384,768]{1,0:T(8,128)(2,1)} %collective-permute-done.28.refs_2_), channel_id=1, source_target_pairs={{0,4},{4,0},{1,5},{5,1},{2,6},{6,2},{3,7},{7,3},{8,12},{12,8},{9,1... | collective-permute-start | bytes 1769480 | tf_op jit(solution)/shard_map/ppermute | solution.py:193
  275.9 144.2 %collective-permute-start.34 = (bf16[384,768]{1,0:T(8,128)(2,1)}, bf16[384,768]{1,0:T(8,128)(2,1)}, u32[]{:S(2)}, u32[]{:S(2)}) collective-permute-start(bf16[384,768]{1,0:T(8,128)(2,1)} %constant_dynamic-update-slice_fusion.6.refs_3_), channel_id=1, source_target_pairs={{0,4},{4,0},{1,5},{5,1},{2,6},{6,2},{3,7},{7,3},{8,12},{12,8},{9,1... | collective-permute-start | bytes 1769480 | tf_op jit(solution)/shard_map/ppermute | solution.py:193
  592.3 29.2 %all-to-all-start.3 = ((bf16[4,160,768]{2,1,0:T(8,128)(2,1)}), bf16[4,160,768]{2,1,0:T(8,128)(2,1)}, u32[]{:S(2)}, u32[]{:S(2)}) async-start(bf16[4,160,768]{2,1,0:T(8,128)(2,1)} %convolution_convert_fusion.3), calls=%async_computation.3 | async-start | bytes 1966080 | tf_op jit(solution)/shard_map/all_to_all | solution.py:517
  607.6 114.1 %collective-permute-start.65 = (bf16[4,96,3072]{2,1,0:T(8,128)(2,1)}, bf16[4,96,3072]{2,1,0:T(8,128)(2,1)}, u32[]{:S(2)}, u32[]{:S(2)}) collective-permute-start(bf16[4,96,3072]{2,1,0:T(8,128)(2,1)} %dynamic-slice_bitcast_fusion.1), channel_id=1, source_target_pairs={{0,4},{4,0},{1,5},{5,1},{2,6},{6,2},{3,7},{7,3},{8,12},{12,8},{9,1... | collective-permute-start | bytes 7077896 | tf_op jit(solution)/shard_map/ppermute | solution.py:193
  621.5 28.3 %all-to-all-start.1 = ((bf16[4,160,768]{2,1,0:T(8,128)(2,1)}), bf16[4,160,768]{2,1,0:T(8,128)(2,1)}, u32[]{:S(2)}, u32[]{:S(2)}) async-start(bf16[4,160,768]{2,1,0:T(8,128)(2,1)} %convolution_convert_fusion.4), calls=%async_computation.1 | async-start | bytes 1966080 | tf_op jit(solution)/shard_map/all_to_all | solution.py:483
  637.2 89.8 %collective-permute-start.71 = (bf16[4,384,768]{2,1,0:T(8,128)(2,1)}, bf16[4,384,768]{2,1,0:T(8,128)(2,1)}, u32[]{:S(2)}, u32[]{:S(2)}) collective-permute-start(bf16[4,384,768]{2,1,0:T(8,128)(2,1)} %dynamic-slice_bitcast_fusion), channel_id=1, source_target_pairs={{0,4},{4,0},{1,5},{5,1},{2,6},{6,2},{3,7},{7,3},{8,12},{12,8},{9,1... | collective-permute-start | bytes 7077896 | tf_op jit(solution)/shard_map/ppermute | solution.py:193
  655.8 36.4 %collective-permute-start.53 = (bf16[4,96,768]{2,1,0:T(8,128)(2,1)S(1)}, bf16[4,96,768]{2,1,0:T(8,128)(2,1)S(1)}, u32[]{:S(2)}, u32[]{:S(2)}) collective-permute-start(bf16[4,96,768]{2,1,0:T(8,128)(2,1)S(1)} %dynamic-slice_bitcast_fusion.3), channel_id=1, source_target_pairs={{0,4},{4,0},{1,5},{5,1},{2,6},{6,2},{3,7},{7,3},{8,12},{12,8},{9,1... | collective-permute-start | bytes 1769480 | tf_op jit(solution)/shard_map/ppermute | solution.py:193
  706.6 47.4 %collective-permute-start.35 = (bf16[512,1536]{1,0:T(8,128)(2,1)}, bf16[512,1536]{1,0:T(8,128)(2,1)}, u32[]{:S(2)}, u32[]{:S(2)}) collective-permute-start(bf16[512,1536]{1,0:T(8,128)(2,1)} %constant_dynamic-slice_fusion.20), channel_id=1, source_target_pairs={{0,4},{4,0},{1,5},{5,1},{2,6},{6,2},{3,7},{7,3},{8,12},{12,8},{9,1... | collective-permute-start | bytes 4718600 | tf_op jit(solution)/shard_map/ppermute | solution.py:193
  731.6 29.5 %collective-permute-start.72 = (bf16[2,384,384]{2,1,0:T(8,128)(2,1)}, bf16[2,384,384]{2,1,0:T(8,128)(2,1)}, u32[]{:S(2)}, u32[]{:S(2)}) collective-permute-start(bf16[2,384,384]{2,1,0:T(8,128)(2,1)} %pad_maximum_fusion.6), channel_id=1, source_target_pairs={{0,8},{8,0},{16,24},{24,16},{1,9},{9,1},{17,25},{25,17},{2,10},{10... | collective-permute-start | bytes 1769480 | tf_op jit(solution)/shard_map/ppermute | solution.py:193
  741.3 44.3 %collective-permute-start.69 = (bf16[96,1536]{1,0:T(8,128)(2,1)}, bf16[96,1536]{1,0:T(8,128)(2,1)}, u32[]{:S(2)}, u32[]{:S(2)}) collective-permute-start(bf16[96,1536]{1,0:T(8,128)(2,1)} %fusion.59), channel_id=1, source_target_pairs={{0,8},{8,0},{16,24},{24,16},{1,9},{9,1},{17,25},{25,17},{2,10},{10... | collective-permute-start | bytes 884744 | tf_op jit(solution)/shard_map/ppermute | solution.py:193
  742.8 44.0 %collective-permute-start.67 = (bf16[96,1536]{1,0:T(8,128)(2,1)}, bf16[96,1536]{1,0:T(8,128)(2,1)}, u32[]{:S(2)}, u32[]{:S(2)}) collective-permute-start(bf16[96,1536]{1,0:T(8,128)(2,1)} %fusion.58), channel_id=1, source_target_pairs={{0,16},{8,24},{16,0},{24,8},{1,17},{9,25},{17,1},{25,9},{2,18},{10... | collective-permute-start | bytes 884744 | tf_op jit(solution)/shard_map/ppermute | solution.py:193
  753.3 34.8 %collective-permute-start.75 = (bf16[384,384]{1,0:T(8,128)(2,1)S(1)}, bf16[384,384]{1,0:T(8,128)(2,1)}, u32[]{:S(2)}, u32[]{:S(2)}) collective-permute-start(bf16[384,384]{1,0:T(8,128)(2,1)S(1)} %fusion.61), channel_id=1, source_target_pairs={{0,8},{8,0},{16,24},{24,16},{1,9},{9,1},{17,25},{25,17},{2,10},{10... | collective-permute-start | bytes 884744 | tf_op jit(solution)/shard_map/ppermute | solution.py:193
  791.4 35.7 %collective-permute-start.76 = (bf16[384,768]{1,0:T(8,128)(2,1)}, bf16[384,768]{1,0:T(8,128)(2,1)}, u32[]{:S(2)}, u32[]{:S(2)}) collective-permute-start(bf16[384,768]{1,0:T(8,128)(2,1)} %pad_maximum_fusion.8), channel_id=1, source_target_pairs={{0,4},{4,0},{1,5},{5,1},{2,6},{6,2},{3,7},{7,3},{8,12},{12,8},{9,1... | collective-permute-start | bytes 1769480 | tf_op jit(solution)/shard_map/ppermute | solution.py:193
  (123 other events, 1082.1 us)
